TPU v7x, 32 devices: a whole 2x2x4 slice. The times are simulated.
32 devices in a mesh: grp: 2 (over y), gz: 4 (over x, core), gx: 4 (over z).
Axes of the slice: x: 2, y: 2, z: 4, core: 2. Of those that a mesh axis runs over, the one named last changes fastest.
Arguments:
- volume: float32 [128, 512, 512], P(('grp', 'gz'), 'gx'), parts along dimension 0, may hold values from -6 to 6
- col_weight: bfloat16 [64, 512, 512], P('gz', 'gx'), may hold values from 0.5 to 2
- column_map: bfloat16 [2, 512, 2048], P(None, 'gx'), may hold values from -0.25 to 0.25
- depth_map: bfloat16 [2, 512, 384], replicated, may hold values from -0.0625 to 0.0625
- measured: float32 [4096, 2, 512], P(('grp', 'gx'), None, 'gz'), parts along dimension 0, may hold values from -6 to 6
- row_weight: float32 [2048, 2, 512], P('gx', None, 'gz'), may hold values from 0.5 to 2
- band_start: int32 [2, 64], P(None, 'gz'), may hold values from 0 to 384, as said below
- band_len: int32 [2, 64], P(None, 'gz'), may hold values from 128 to 384, as said below
Outputs:
- updated_volume: float32 [128, 512, 512], P(('grp', 'gz'), 'gx'), parts along dimension 0
There are 2 independent parts, one for each index of `grp`. A program takes and returns all parts, laid end to end along the dimension named above; an argument that names none is the same for every part. Nothing has to cross between parts.
Inputs may be any that keep to these rules, and one draw needn't show every extreme that they name: `band_start`: A multiple of 128. For a slice of group g (slices 16 * g to 16 * (g + 1) - 1) it is 128 * (g - 1) or 128 * g, never negative. `band_len`: A multiple of 128. The band of a slice of group g covers detector rows 128 * g to 128 * (g + 1) - 1 and ends at or before row 128 * (g + 2) and at or before row 512.
All inputs are finite; a program needn't handle non-finite values.
Results may differ from a plain program's by a relative error of at most 0.0046.
Values may be sent and summed in bfloat16 or wider, within the bound.
A program may use at most 64 MiB of HBM per device.

v0:
```python
import jax
import jax.numpy as jnp
from jax import lax
from jax.sharding import PartitionSpec as P

BLK = 128
WIN = 384


def from_behind(block, axis, distance):
    devices = range(lax.axis_size(axis))
    route = [(i - distance, i) for i in devices if i - distance in devices]
    return lax.ppermute(block, axis, route)


def local(volume, col_weight, column_map, depth_map, measured, row_weight, band_start, band_len):
    slices, x_columns, y_cells = volume.shape
    view_count = depth_map.shape[0]
    group_index = lax.axis_index("gz")
    shifted = band_start - (group_index - 1) * BLK == BLK
    row_index = jnp.arange(WIN, dtype=jnp.int32)
    in_band = row_index[None, None, :] < band_len[:, :, None]
    coarse = volume.astype(jnp.bfloat16)
    windows = []
    for which_view in range(view_count):
        footprint = jnp.einsum(
            "zxy,yt->zxt", coarse, depth_map[which_view], preferred_element_type=jnp.float32
        )
        footprint = jnp.where(in_band[which_view][:, None, :], footprint, 0.0)
        first_part = jnp.sum(jnp.where(shifted[which_view][:, None, None], 0.0, footprint), axis=0)
        second_part = jnp.sum(jnp.where(shifted[which_view][:, None, None], footprint, 0.0), axis=0)
        second_part = jnp.concatenate(
            [jnp.zeros((x_columns, BLK), jnp.float32), second_part[:, : WIN - BLK]], axis=1
        )
        windows.append(first_part + second_part)
    detector_frame = jnp.stack(windows).astype(jnp.bfloat16)
    column_portion = column_map
    column_share = lax.psum_scatter(
        jnp.einsum(
            "piu,pit->upt", column_portion, detector_frame, preferred_element_type=jnp.float32
        ),
        "gx",
        scatter_dimension=0,
        tiled=True,
    )
    from_lower = from_behind(column_share[:, :, 2 * BLK :], "gz", 1)
    from_upper = from_behind(column_share[:, :, :BLK], "gz", -1)
    owned_rows = column_share[:, :, BLK : 2 * BLK] + from_lower + from_upper
    residual = (row_weight * (measured - owned_rows)).astype(jnp.bfloat16)
    below_rows = from_behind(residual, "gz", 1)
    above_rows = from_behind(residual, "gz", -1)
    band_rows = jnp.concatenate([below_rows, residual, above_rows], axis=2)
    column_portion = column_map
    distribute_rays = jnp.einsum(
        "phr,rpk->phk",
        column_portion,
        lax.all_gather(band_rows, "gx", axis=0, tiled=True),
        preferred_element_type=jnp.float32,
    )
    distribute_rays = distribute_rays.astype(jnp.bfloat16)
    backprojected = jnp.zeros((slices, x_columns, y_cells), jnp.float32)
    for which_view in range(view_count):
        advanced = jnp.concatenate(
            [distribute_rays[which_view][:, BLK:], jnp.zeros((x_columns, BLK), jnp.bfloat16)],
            axis=1,
        )
        chosen = jnp.where(
            shifted[which_view][:, None, None], advanced[None], distribute_rays[which_view][None]
        )
        chosen = jnp.where(in_band[which_view][:, None, :], chosen, jnp.zeros((), jnp.bfloat16))
        backprojected = backprojected + jnp.einsum(
            "zxt,yt->zxy", chosen, depth_map[which_view], preferred_element_type=jnp.float32
        )
    return volume + col_weight.astype(jnp.float32) * backprojected


def solution(mesh):
    in_specs = (
        P(("grp", "gz"), "gx", None),
        P("gz", "gx", None),
        P(None, "gx", None),
        P(),
        P(("grp", "gx"), None, "gz"),
        P("gx", None, "gz"),
        P(None, "gz"),
        P(None, "gz"),
    )
    out_specs = P(("grp", "gz"), "gx", None)
    return jax.shard_map(local, mesh=mesh, in_specs=in_specs, out_specs=out_specs, check_vma=False)
```

profile of v0, /device:TPU:1, one launch (start us, length us, event | category | flops | bytes accessed | tf_op | source)
XLA Modules:
  0.0 242.3 jit_solution(3323715548053582774)
XLA Ops:
  6.5 0.0 copy-start
  6.5 0.0 reduce-scatter.2.cloned.1.call-start
  6.5 0.8 iota_compare_fusion
  7.4 0.7 subtract_compare_fusion
  8.1 0.0 copy-start.5
  8.1 3.8 %select_reduce_fusion.2 = (f32[128,384]{1,0:T(8,128)S(1)}, f32[128,384]{1,0:T(8,128)S(1)}) fusion(pred[16]{0:T(512)(128)(4,1)S(1)} %get-tuple-element.16, pred[16,384]{1,0:T(8,128)(4,1)S(1)} %get-tuple-element.14, bf16[2,512,384]{2,1,0:T(8,128)(2,1)} %param.11, f32[16,128,512]{2,1,0:T(8,128)} %param.8), kind=kOutput, calls=%fused_computation.4 | convolution fusion | flops 810188800 | bytes 4986896 | tf_op jit(solution)/shard_map/zxy,yt->zxt/dot_general | solution.py:26
  11.9 0.1 copy.25
  12.0 0.0 copy-done.5
  12.0 3.6 %select_reduce_fusion = (f32[128,384]{1,0:T(8,128)S(1)}, f32[128,384]{1,0:T(8,128)S(1)}) fusion(pred[16]{0:T(512)(128)(4,1)S(1)} %get-tuple-element.15, pred[16,384]{1,0:T(8,128)(4,1)S(1)} %get-tuple-element.13, bf16[2,512,384]{2,1,0:T(8,128)(2,1)S(1)} %copy-done.5, f32[16,128,512]{2,1,0:T(8,128)} %param.8), kind=kOutput, calls=%fused_computation.2 | convolution fusion | flops 810188800 | bytes 4987392 | tf_op jit(solution)/shard_map/zxy,yt->zxt/dot_general | solution.py:26
  15.6 0.1 copy.26
  15.7 0.1 copy.16
  15.9 0.1 copy.18
  16.1 0.0 copy-done
  16.1 3.6 %convolution_bitcast_fusion = f32[2048,2,384]{0,2,1:T(8,128)} fusion(bf16[2,128,2048]{2,1,0:T(8,128)(2,1)S(1)} %copy-done, bf16[1,128,384]{1,2,0:T(8,128)(2,1)S(1)} %get-tuple-element.18, bf16[1,128,384]{1,2,0:T(8,128)(2,1)S(1)} %get-tuple-element.17), kind=kOutput, calls=%fused_computation.1 | convolution fusion | flops 402751488 | bytes 7536640 | tf_op jit(solution)/shard_map/piu,pit->upt/dot_general | solution.py:39
  19.7 0.0 copy-start.3
  19.7 0.0 reduce-scatter.2.cloned.1.call-update
  19.7 0.0 copy-start.4
  19.7 0.0 all-gather.2.cloned.1.call-start
  19.8 113.0 %reduce-scatter.2.cloned.1.call-done = f32[512,2,384]{0,2,1:T(8,128)} async-done(((f32[2048,2,384]{0,2,1:T(8,128)}), f32[512,2,384]{0,2,1:T(8,128)}) %reduce-scatter.2.cloned.1.call-update) | async-done | bytes 1572880 | tf_op jit(solution)/shard_map/reduce_scatter | solution.py:38
  132.8 2.2 fusion.40
  135.0 3.6 %collective-permute-start = (f32[512,2,128]{0,2,1:T(8,128)}, f32[512,2,128]{0,2,1:T(8,128)S(1)}, u32[]{:S(2)}, u32[]{:S(2)}) collective-permute-start(f32[512,2,128]{0,2,1:T(8,128)} %get-tuple-element.9), channel_id=1, source_target_pairs={{0,4},{4,8},{8,12},{1,5},{5,9},{9,13},{2,6},{6,10},{10,14},{3,7},{... | collective-permute-start | bytes 1572872 | tf_op jit(solution)/shard_map/ppermute | solution.py:13
  138.6 1.9 collective-permute-start.1
  140.5 0.0 copy-done.3
  140.5 0.2 copy.19
  140.8 0.0 copy-done.4
  140.8 0.2 copy.20
  141.0 4.0 %collective-permute-done = f32[512,2,128]{0,2,1:T(8,128)S(1)} collective-permute-done((f32[512,2,128]{0,2,1:T(8,128)}, f32[512,2,128]{0,2,1:T(8,128)S(1)}, u32[]{:S(2)}, u32[]{:S(2)}) %collective-permute-start) | collective-permute-done | bytes 524320 | tf_op jit(solution)/shard_map/ppermute | solution.py:13
  145.0 4.4 %collective-permute-done.1 = f32[512,2,128]{0,2,1:T(8,128)} collective-permute-done((f32[512,2,128]{0,2,1:T(8,128)}, f32[512,2,128]{0,2,1:T(8,128)}, u32[]{:S(2)}, u32[]{:S(2)}) %collective-permute-start.1) | collective-permute-done | bytes 524320 | tf_op jit(solution)/shard_map/ppermute | solution.py:13
  149.4 1.4 fusion.23
  150.9 1.9 collective-permute-start.2
  152.8 2.4 collective-permute-start.3
  155.2 0.9 collective-permute-done.2
  156.1 4.4 %collective-permute-done.3 = bf16[512,2,128]{0,2,1:T(8,128)(2,1)S(1)} collective-permute-done((bf16[512,2,128]{0,2,1:T(8,128)(2,1)S(1)}, bf16[512,2,128]{0,2,1:T(8,128)(2,1)S(1)}, u32[]{:S(2)}, u32[]{:S(2)}) %collective-permute-start.3) | collective-permute-done | bytes 262176 | tf_op jit(solution)/shard_map/ppermute | solution.py:13
  160.5 0.9 pad_maximum_fusion
  161.4 0.0 all-gather.2.cloned.1.call-update
  161.4 62.7 %all-gather.2.cloned.1.call-done = bf16[2048,2,384]{0,2,1:T(8,128)(2,1)} async-done(((bf16[512,2,384]{0,2,1:T(8,128)(2,1)}), bf16[2048,2,384]{0,2,1:T(8,128)(2,1)}) %all-gather.2.cloned.1.call-update) | async-done | bytes 3145744 | tf_op jit(solution)/shard_map/all_gather | solution.py:57
  224.2 2.9 %fusion.9 = bf16[2,128,384]{1,2,0:T(8,128)(2,1)S(1)} fusion(bf16[2048,2,384]{0,2,1:T(8,128)(2,1)} %all-gather.2.cloned.1.call-done, bf16[2,128,2048]{2,1,0:T(8,128)(2,1)S(1)} %copy-done), kind=kOutput, calls=%fused_computation.16 | convolution fusion | flops 402751488 | bytes 4390912 | tf_op jit(solution)/shard_map/phr,rpk->phk/dot_general | solution.py:54
  227.1 0.8 copy.22
  227.8 0.1 copy.24
  227.9 0.0 copy-start.2
  228.0 0.1 copy.27
  228.1 0.1 copy.28
  228.2 0.0 copy-start.1
  228.2 2.5 %fusion.2 = f32[16,128,512]{2,1,0:T(8,128)S(1)} fusion(pred[16]{0:T(512)(128)(4,1)S(1)} %get-tuple-element.16, pred[16,384]{1,0:T(8,128)(4,1)S(1)} %get-tuple-element.14, bf16[128,384]{1,0:T(8,128)(2,1)} %copy.22, bf16[128,384]{1,0:T(8,128)(2,1)S(1)} %concatenate.18.clone, bf16[2,512,384]{2,1,0:T(8,128)(2,1)} %param.11), kind=kOutput, calls=%fused_computation.8 | convolution fusion | flops 806879232 | bytes 4790288 | tf_op jit(solution)/shard_map/zxt,yt->zxy/dot_general | solution.py:71
  230.8 0.0 copy-done.2
  230.8 0.2 copy-done.1
  231.0 4.5 %multiply_add_fusion = f32[16,128,512]{2,1,0:T(8,128)} fusion(f32[16,128,512]{2,1,0:T(8,128)S(1)} %copy-done.1, f32[16,128,512]{2,1,0:T(8,128)S(1)} %fusion.2, bf16[16,128,512]{2,1,0:T(8,128)(2,1)S(1)} %copy-done.2, pred[16]{0:T(512)(128)(4,1)S(1)} %get-tuple-element.15, pred[16,384]{1,0:T(8,128)(4,1)S(1)} %get-tuple-element.13, ...), kind=kOutput, calls=%fused_computation | convolution fusion | flops 811073536 | bytes 15276048 | tf_op jit(solution)/shard_map/zxt,yt->zxy/dot_general | solution.py:71
  (10 shorter events, 0.1 us)
Async XLA Ops:
  6.5 9.5 %copy-start = (bf16[2,128,2048]{2,1,0:T(8,128)(2,1)S(1)}, bf16[2,128,2048]{2,1,0:T(8,128)(2,1)}, u32[]{:S(2)}) copy-start(bf16[2,128,2048]{2,1,0:T(8,128)(2,1)} %param.10) | copy-start | bytes 3145732
  6.5 126.2 %reduce-scatter.2.cloned.1.call-start = ((), (), s32[]{:S(2)}) async-start(), calls=%async_computation.1 | async-start | bytes 7864320 | tf_op jit(solution)/shard_map/reduce_scatter | solution.py:38
  8.1 3.9 %copy-start.5 = (bf16[2,512,384]{2,1,0:T(8,128)(2,1)S(1)}, bf16[2,512,384]{2,1,0:T(8,128)(2,1)}, u32[]{:S(2)}) copy-start(bf16[2,512,384]{2,1,0:T(8,128)(2,1)} %param.11) | copy-start | bytes 2359300
  19.7 120.8 %copy-start.3 = (f32[512,2,128]{2,1,0:T(2,128)S(1)}, f32[512,2,128]{2,1,0:T(2,128)}, u32[]{:S(2)}) copy-start(f32[512,2,128]{2,1,0:T(2,128)} %param.12) | copy-start | bytes 1572868
  19.7 121.0 %copy-start.4 = (f32[512,2,128]{2,1,0:T(2,128)S(1)}, f32[512,2,128]{2,1,0:T(2,128)}, u32[]{:S(2)}) copy-start(f32[512,2,128]{2,1,0:T(2,128)} %param.13) | copy-start | bytes 1572868
  19.7 204.4 %all-gather.2.cloned.1.call-start = ((), (), s32[]{:S(2)}) async-start(), calls=%async_computation.2 | async-start | bytes 3932160 | tf_op jit(solution)/shard_map/all_gather | solution.py:57
  135.0 10.0 %collective-permute-start = (f32[512,2,128]{0,2,1:T(8,128)}, f32[512,2,128]{0,2,1:T(8,128)S(1)}, u32[]{:S(2)}, u32[]{:S(2)}) collective-permute-start(f32[512,2,128]{0,2,1:T(8,128)} %get-tuple-element.9), channel_id=1, source_target_pairs={{0,4},{4,8},{8,12},{1,5},{5,9},{9,13},{2,6},{6,10},{10,14},{3,7},{... | collective-permute-start | bytes 1572872 | tf_op jit(solution)/shard_map/ppermute | solution.py:13
  138.6 10.8 %collective-permute-start.1 = (f32[512,2,128]{0,2,1:T(8,128)}, f32[512,2,128]{0,2,1:T(8,128)}, u32[]{:S(2)}, u32[]{:S(2)}) collective-permute-start(f32[512,2,128]{0,2,1:T(8,128)} %get-tuple-element.10), channel_id=1, source_target_pairs={{4,0},{8,4},{12,8},{5,1},{9,5},{13,9},{6,2},{10,6},{14,10},{7,3},{... | collective-permute-start | bytes 1572872 | tf_op jit(solution)/shard_map/ppermute | solution.py:13
  150.9 5.2 %collective-permute-start.2 = (bf16[512,2,128]{0,2,1:T(8,128)(2,1)S(1)}, bf16[512,2,128]{0,2,1:T(8,128)(2,1)S(1)}, u32[]{:S(2)}, u32[]{:S(2)}) collective-permute-start(bf16[512,2,128]{0,2,1:T(8,128)(2,1)S(1)} %fusion.23), channel_id=1, source_target_pairs={{0,4},{4,8},{8,12},{1,5},{5,9},{9,13},{2,6},{6,10},{10,14},{3,7},{... | collective-permute-start | bytes 786440 | tf_op jit(solution)/shard_map/ppermute | solution.py:13
  152.8 7.7 %collective-permute-start.3 = (bf16[512,2,128]{0,2,1:T(8,128)(2,1)S(1)}, bf16[512,2,128]{0,2,1:T(8,128)(2,1)S(1)}, u32[]{:S(2)}, u32[]{:S(2)}) collective-permute-start(bf16[512,2,128]{0,2,1:T(8,128)(2,1)S(1)} %fusion.23), channel_id=1, source_target_pairs={{4,0},{8,4},{12,8},{5,1},{9,5},{13,9},{6,2},{10,6},{14,10},{7,3},{... | collective-permute-start | bytes 786440 | tf_op jit(solution)/shard_map/ppermute | solution.py:13
  227.9 2.8 %copy-start.2 = (bf16[16,128,512]{2,1,0:T(8,128)(2,1)S(1)}, bf16[16,128,512]{2,1,0:T(8,128)(2,1)}, u32[]{:S(2)}) copy-start(bf16[16,128,512]{2,1,0:T(8,128)(2,1)} %param.9) | copy-start | bytes 6291460
  228.2 2.8 %copy-start.1 = (f32[16,128,512]{2,1,0:T(8,128)S(1)}, f32[16,128,512]{2,1,0:T(8,128)}, u32[]{:S(2)}) copy-start(f32[16,128,512]{2,1,0:T(8,128)} %param.8) | copy-start | bytes 12582916
Sparse Core Ops, SparseCore 0:
  19.9 112.8 reduce-scatter.1
  161.6 62.5 all-gather.1
where the time goes:
time: 243 us; the launch traced here: 242 us
  waiting for transfers between devices  189 us (78%)
  matrix products  20.9 us (9%)
  between operations  13.7 us (6%)
  starting transfers between devices  9.88 us (4%)
  local copies, waits for them, and re-layouts  4.53 us (2%)
  other arithmetic  3.93 us (2%)
    reduce_scatter x1, waiting for transfers between devices, local(): lax.psum_scatter(jnp.einsum('piu,pit->upt', column_portion, detector_fram...  113 us
    all_gather x1, waiting for transfers between devices, local(): lax.all_gather(band_rows, 'gx', axis=0, tiled=True)  62.7 us
    ppermute x4, waiting for transfers between devices, from_behind(): return lax.ppermute(block, axis, route)  13.7 us
    ppermute x4, starting transfers between devices, from_behind(): return lax.ppermute(block, axis, route)  9.83 us
    dot_general x2, matrix products, local(): jnp.einsum('zxy,yt->zxt', coarse, depth_map[which_view], preferred_elemen...  7.38 us
    dot_general x2, matrix products, local(): jnp.einsum('zxt,yt->zxy', chosen, depth_map[which_view], preferred_elemen...  6.99 us
  transfers between devices with their start and end apart: 6, of which 6 were waited for; matrix products, arithmetic and copies ran while one was open for 0% of the time, Pallas kernels for 0%

commit v1 on v0

v1 whole, which is shorter than its diff:
```python
import functools

import jax
import jax.numpy as jnp
from jax import lax
from jax.experimental import pallas as pl
from jax.experimental.pallas import tpu as pltpu
from jax.sharding import PartitionSpec as P

BLK = 128
VIEWS = 2
CHUNK = 4
MESH = pl.DeviceIdType.MESH
BF16 = jnp.bfloat16
F32 = jnp.float32


def middle_kernel(
    n, groups,
    start_ref, len_ref, volume, depth, colmap, measured, weight,
    out_ref,
    vol, dcat, maps, meas, rw, meas_t, rw_t, acc, wt, halo, gathered, part, parts_in, own, halo_s,
    vol_sem, dep_sem, loc_sem,
    m_send, m_recv, f_send, f_recv, h_send, h_recv, g_send, g_recv, r_send, r_recv, s_send, s_recv,
):
    g = lax.axis_index("gz")
    me = lax.axis_index("gx")
    core = lax.rem(g, 2)
    sibling = g + 1 - 2 * core
    cols = maps.shape[2]
    slices = vol.shape[0]
    steps = slices // CHUNK
    t_len = depth.shape[2]

    def my_columns(who):
        return pl.ds(pl.multiple_of(who * cols, 128), cols)

    def x_rows(who):
        return pl.ds(pl.multiple_of(who * BLK, BLK), BLK)

    depth_copies = [
        pltpu.make_async_copy(depth.at[v], dcat.at[:, pl.ds(v * t_len, t_len)], dep_sem.at[v])
        for v in range(VIEWS)
    ]
    for copy in depth_copies:
        copy.start()

    def vol_copy(k):
        return pltpu.make_async_copy(
            volume.at[pl.ds(k * CHUNK, CHUNK)], vol.at[pl.ds(k * CHUNK, CHUNK)], vol_sem.at[k]
        )

    for k in range(steps):
        vol_copy(k).start()
    local_copies = [
        pltpu.make_async_copy(colmap.at[:, :, my_columns(me)], maps.at[:, x_rows(me), :], loc_sem.at[0]),
        pltpu.make_async_copy(measured, meas, loc_sem.at[1]),
        pltpu.make_async_copy(weight, rw, loc_sem.at[2]),
    ]
    for copy in local_copies:
        copy.start()

    barrier = pltpu.get_barrier_semaphore()
    for d in range(1, n):
        pl.semaphore_signal(barrier, inc=1, device_id={"gx": lax.rem(me + d, n)}, device_id_type=MESH)

    @pl.when(g > 0)
    def _():
        pl.semaphore_signal(barrier, inc=1, device_id={"gz": g - 1}, device_id_type=MESH)

    @pl.when(g < groups - 1)
    def _():
        pl.semaphore_signal(barrier, inc=1, device_id={"gz": g + 1}, device_id_type=MESH)

    below = jnp.where(g > 0, 1, 0)
    above = jnp.where(g < groups - 1, 1, 0)
    pl.semaphore_wait(barrier, n - 1 + below + above)

    def map_copy(d):
        peer = lax.rem(me + d, n)
        return pltpu.make_async_remote_copy(
            src_ref=colmap.at[core, :, my_columns(peer)],
            dst_ref=maps.at[core, x_rows(me), :],
            send_sem=m_send.at[d], recv_sem=m_recv.at[d],
            device_id={"gx": peer}, device_id_type=MESH,
        )

    for d in range(1, n):
        map_copy(d).start()

    acc[...] = jnp.zeros_like(acc)
    for copy in depth_copies:
        copy.wait()

    def forward(k, carry):
        vol_copy(k).wait()
        coarse = vol[pl.ds(k * CHUNK, CHUNK)].astype(BF16).reshape(CHUNK * BLK, vol.shape[2])
        foot = jnp.dot(coarse, dcat[...], preferred_element_type=F32)
        for v in range(VIEWS):
            sums = [acc[v, b] for b in range(3)]
            for i in range(CHUNK):
                z = k * CHUNK + i
                low = jnp.where(start_ref[v, z] < g * BLK, 1.0, 0.0).astype(F32)
                up = jnp.where(start_ref[v, z] + len_ref[v, z] > (g + 1) * BLK, 1.0, 0.0).astype(F32)
                t = [
                    foot[i * BLK:(i + 1) * BLK, v * t_len + b * BLK:v * t_len + (b + 1) * BLK]
                    for b in range(3)
                ]
                sums[0] = sums[0] + low * t[0]
                sums[1] = sums[1] + low * t[1] + (1.0 - low) * t[0]
                sums[2] = sums[2] + (low * up) * t[2] + ((1.0 - low) * up) * t[1]
            for b in range(3):
                acc[v, b] = sums[b]
        return carry

    lax.fori_loop(0, steps, forward, 0)
    for b in (0, 2):
        for v in range(VIEWS):
            wt[b // 2, v] = acc[v, b].T.astype(BF16)

    def to_below(src, dst, send, recv):
        return pltpu.make_async_remote_copy(
            src_ref=src, dst_ref=dst, send_sem=send.at[0], recv_sem=recv.at[0],
            device_id={"gz": g - 1}, device_id_type=MESH,
        )

    def to_above(src, dst, send, recv):
        return pltpu.make_async_remote_copy(
            src_ref=src, dst_ref=dst, send_sem=send.at[1], recv_sem=recv.at[1],
            device_id={"gz": g + 1}, device_id_type=MESH,
        )

    def exchange_start(low_src, high_src, land, send, recv):
        @pl.when(g > 0)
        def _():
            to_below(low_src, land.at[1], send, recv).start()

        @pl.when(g < groups - 1)
        def _():
            to_above(high_src, land.at[0], send, recv).start()

        @pl.when(g == 0)
        def _():
            land[0] = jnp.zeros_like(land[0])

        @pl.when(g == groups - 1)
        def _():
            land[1] = jnp.zeros_like(land[1])

    def exchange_wait(low_src, high_src, land, send, recv):
        @pl.when(g > 0)
        def _():
            to_below(low_src, land.at[1], send, recv).wait_send()
            to_above(high_src, land.at[0], send, recv).wait_recv()

        @pl.when(g < groups - 1)
        def _():
            to_above(high_src, land.at[0], send, recv).wait_send()
            to_below(low_src, land.at[1], send, recv).wait_recv()

    exchange_start(wt.at[0], wt.at[1], halo, h_send, h_recv)
    for copy in local_copies:
        copy.wait()
    for v in range(VIEWS):
        meas_t[v] = meas[pl.ds(v, cols, stride=VIEWS), :].T
        rw_t[v] = rw[pl.ds(v, cols, stride=VIEWS), :].T
    middle = [acc[v, 1].T.astype(BF16).astype(F32) for v in range(VIEWS)]
    exchange_wait(wt.at[0], wt.at[1], halo, h_send, h_recv)
    for v in range(VIEWS):
        total = middle[v] + halo[0, v].astype(F32) + halo[1, v].astype(F32)
        gathered[me, v] = total.astype(BF16)

    def gather_copy(d, slot):
        return pltpu.make_async_remote_copy(
            src_ref=gathered.at[slot], dst_ref=gathered.at[slot],
            send_sem=g_send.at[d], recv_sem=g_recv.at[d],
            device_id={"gx": lax.rem(me + d, n)}, device_id_type=MESH,
        )

    for d in range(1, n):
        gather_copy(d, me).start()

    def forward_copy(d, view):
        src = lax.rem(me - d + n, n)
        return pltpu.make_async_remote_copy(
            src_ref=maps.at[view, x_rows(src), :], dst_ref=maps.at[view, x_rows(src), :],
            send_sem=f_send.at[d], recv_sem=f_recv.at[d],
            device_id={"gz": sibling}, device_id_type=MESH,
        )

    for d in range(1, n):
        map_copy(d).wait_recv()
        forward_copy(d, core).start()
    for d in range(1, n):
        gather_copy(d, lax.rem(me - d + n, n)).wait_recv()
    for d in range(1, n):
        forward_copy(d, 1 - core).wait_recv()

    own_parts = []
    for v in range(VIEWS):
        window = jnp.concatenate([gathered[j, v] for j in range(n)], axis=1)
        projection = jnp.dot(window, maps[v], preferred_element_type=F32)
        residual = (rw_t[v] * (meas_t[v] - projection)).astype(BF16)
        spread = lax.dot_general(residual, maps[v], (((1,), (1,)), ((), ())), preferred_element_type=F32)
        for j in range(n):
            own[j, v] = spread[:, j * BLK:(j + 1) * BLK]
            part[j, v] = spread[:, j * BLK:(j + 1) * BLK].astype(BF16)

    def reduce_copy(d):
        peer = lax.rem(me + d, n)
        return pltpu.make_async_remote_copy(
            src_ref=part.at[peer], dst_ref=parts_in.at[d],
            send_sem=r_send.at[d], recv_sem=r_recv.at[d],
            device_id={"gx": peer}, device_id_type=MESH,
        )

    for d in range(1, n):
        reduce_copy(d).start()
    totals = [own[me, v] for v in range(VIEWS)]
    for d in range(1, n):
        reduce_copy(d).wait_recv()
        totals = [totals[v] + parts_in[d, v].astype(F32) for v in range(VIEWS)]
    for v in range(VIEWS):
        halo_s[2, v] = totals[v].T.astype(BF16)

    exchange_start(halo_s.at[2], halo_s.at[2], halo_s, s_send, s_recv)
    out_ref[1] = halo_s[2]
    exchange_wait(halo_s.at[2], halo_s.at[2], halo_s, s_send, s_recv)
    out_ref[0] = halo_s[0]
    out_ref[2] = halo_s[1]
    for d in range(1, n):
        map_copy(d).wait_send()
        gather_copy(d, me).wait_send()
        forward_copy(d, core).wait_send()
        reduce_copy(d).wait_send()


def middle(volume, column_map, depth_map, measured, row_weight, band_start, band_len):
    n, groups = lax.axis_size("gx"), lax.axis_size("gz")
    slices, x_columns, y_cells = volume.shape
    views, _, t_len = depth_map.shape
    cols = measured.shape[0]
    hbm = pl.BlockSpec(memory_space=pl.ANY)
    smem = pl.BlockSpec(memory_space=pltpu.SMEM)
    block = (views, BLK, BLK)
    dma = pltpu.SemaphoreType.DMA
    return pl.pallas_call(
        functools.partial(middle_kernel, n, groups),
        out_shape=jax.ShapeDtypeStruct((3, *block), BF16),
        in_specs=[smem, smem, hbm, hbm, hbm, hbm, hbm],
        out_specs=pl.BlockSpec(memory_space=pltpu.VMEM),
        scratch_shapes=[
            pltpu.VMEM((slices, x_columns, y_cells), F32),
            pltpu.VMEM((y_cells, views * t_len), BF16),
            pltpu.VMEM((views, n * BLK, cols), BF16),
            pltpu.VMEM((cols * views, BLK), F32),
            pltpu.VMEM((cols * views, BLK), F32),
            pltpu.VMEM((views, BLK, cols), F32),
            pltpu.VMEM((views, BLK, cols), F32),
            pltpu.VMEM((views, 3, BLK, BLK), F32),
            pltpu.VMEM((2, *block), BF16),
            pltpu.VMEM((2, *block), BF16),
            pltpu.VMEM((n, *block), BF16),
            pltpu.VMEM((n, *block), BF16),
            pltpu.VMEM((n, *block), BF16),
            pltpu.VMEM((n, *block), F32),
            pltpu.VMEM((3, *block), BF16),
            dma((slices // CHUNK,)), dma((views,)), dma((3,)),
            dma((n,)), dma((n,)), dma((n,)), dma((n,)), dma((2,)), dma((2,)),
            dma((n,)), dma((n,)), dma((n,)), dma((n,)), dma((2,)), dma((2,)),
        ],
        compiler_params=pltpu.CompilerParams(
            collective_id=0, has_side_effects=True, vmem_limit_bytes=32 * 1024 * 1024
        ),
        name="project_and_spread",
    )(
        band_start, band_len, volume, depth_map, column_map,
        measured.reshape(cols * views, BLK), row_weight.reshape(cols * views, BLK),
    )


def back_kernel(start_ref, len_ref, spread, depth, volume, col_weight, out_ref, images):
    g = lax.axis_index("gz")
    step = pl.program_id(0)
    depth_contract = (((1,), (1,)), ((), ()))

    @pl.when(step == 0)
    def _():
        for v in range(VIEWS):
            low = jnp.concatenate([spread[0, v], spread[1, v]], axis=1)
            high = jnp.concatenate([spread[1, v], spread[2, v]], axis=1)
            pair = lax.dot_general(
                jnp.concatenate([low, high], axis=0), depth[v, :, :2 * BLK],
                depth_contract, preferred_element_type=F32,
            )
            images[v, 0] = lax.dot_general(
                spread[1, v], depth[v, :, :BLK], depth_contract, preferred_element_type=F32
            )
            images[v, 1] = pair[:BLK]
            images[v, 2] = pair[BLK:]
            images[v, 3] = pair[:BLK] + lax.dot_general(
                spread[2, v], depth[v, :, 2 * BLK:], depth_contract, preferred_element_type=F32
            )

    count = volume.shape[0]
    for i in range(count):
        z = step * count + i
        total = None
        for v in range(VIEWS):
            low = (start_ref[v, z] < g * BLK).astype(jnp.int32)
            up = (start_ref[v, z] + len_ref[v, z] > (g + 1) * BLK).astype(jnp.int32)
            image = images[v, low + 2 * up]
            total = image if total is None else total + image
        out_ref[i] = volume[i] + col_weight[i].astype(F32) * total


def back(spread, depth_map, volume, col_weight, band_start, band_len):
    slices, x_columns, y_cells = volume.shape
    count = 2
    smem = pl.BlockSpec(memory_space=pltpu.SMEM)
    slab = pl.BlockSpec((count, x_columns, y_cells), lambda i: (i, 0, 0))
    return pl.pallas_call(
        back_kernel,
        grid=(slices // count,),
        out_shape=jax.ShapeDtypeStruct(volume.shape, F32),
        in_specs=[
            smem, smem,
            pl.BlockSpec(spread.shape, lambda i: (0, 0, 0, 0)),
            pl.BlockSpec(depth_map.shape, lambda i: (0, 0, 0)),
            slab, slab,
        ],
        out_specs=slab,
        scratch_shapes=[pltpu.VMEM((VIEWS, 4, x_columns, y_cells), F32)],
        compiler_params=pltpu.CompilerParams(vmem_limit_bytes=32 * 1024 * 1024),
        name="backproject",
    )(band_start, band_len, spread, depth_map, volume, col_weight)


def local(volume, col_weight, column_map, depth_map, measured, row_weight, band_start, band_len):
    spread = middle(volume, column_map, depth_map, measured, row_weight, band_start, band_len)
    return back(spread, depth_map, volume, col_weight, band_start, band_len)


def solution(mesh):
    in_specs = (
        P(("grp", "gz"), "gx", None),
        P("gz", "gx", None),
        P(None, "gx", None),
        P(),
        P(("grp", "gx"), None, "gz"),
        P("gx", None, "gz"),
        P(None, "gz"),
        P(None, "gz"),
    )
    out_specs = P(("grp", "gz"), "gx", None)
    return jax.shard_map(local, mesh=mesh, in_specs=in_specs, out_specs=out_specs, check_vma=False)
```

time: 243 us -> 47.2 us (0.19)
  waiting for transfers between devices: 189 us -> 0 us
  Pallas kernels: 0 us -> 38.9 us
  matrix products: 20.9 us -> 0 us
  between operations: 13.7 us -> 0.02 us
  starting transfers between devices: 9.88 us -> 0 us
  other arithmetic: 3.93 us -> 0 us
  local copies, waits for them, and re-layouts: 4.53 us -> 7.99 us
    reduce_scatter x1 -> x0, waiting for transfers between devices: 113 us -> none  [local(): lax.psum_scatter(jnp.einsum('piu,pit->upt', column_portion, detector_fram...]
    all_gather x1 -> x0, waiting for transfers between devices: 62.7 us -> none  [local(): lax.all_gather(band_rows, 'gx', axis=0, tiled=True)]
    pallas_call x0 -> x2, Pallas kernels: none -> 38.9 us  [the longest x1 33.7 us: middle(): pl.pallas_call(functools.partial(middle_kernel, n, groups), out_shape=jax...]
    dot_general x6 -> x0, matrix products: 20.9 us -> none  [the longest x2 7.38 us: local(): jnp.einsum('zxy,yt->zxt', coarse, depth_map[which_view], preferred_elemen...]
    ppermute x4 -> x0, waiting for transfers between devices: 13.7 us -> none  [from_behind(): return lax.ppermute(block, axis, route)]
    ppermute x4 -> x0, starting transfers between devices: 9.83 us -> none  [from_behind(): return lax.ppermute(block, axis, route)]
    unnamed x18 -> x16, local copies, waits for them, and re-layouts: 1.07 us -> 7.99 us
  transfers between devices with their start and end apart: 6 -> 0, of which waited for: 6 -> 0; matrix products, arithmetic and copies ran while one was open for 0% -> 0% of each run, Pallas kernels for 0% -> 0%
where the time goes in v1:
time: 47.2 us; the launch traced here: 46.9 us
  Pallas kernels  38.9 us (82%)
  local copies, waits for them, and re-layouts  7.99 us (17%)
    pallas_call x1, Pallas kernels, middle(): pl.pallas_call(functools.partial(middle_kernel, n, groups), out_shape=jax...  33.7 us
    unnamed x16, local copies, waits for them, and re-layouts  7.99 us
    pallas_call x1, Pallas kernels, back(): pl.pallas_call(back_kernel, grid=(slices // count,), out_shape=jax.ShapeD...  5.11 us

profile of v1, /device:TPU:1, one launch (start us, length us, event | category | flops | bytes accessed | tf_op | source)
XLA Modules:
  0.0 46.9 jit_solution(11016332117476942503)
XLA Ops:
  0.0 0.0 copy-start
  0.0 2.2 %copy-done = f32[16,128,512]{2,1,0:T(8,128)S(1)} copy-done((f32[16,128,512]{2,1,0:T(8,128)S(1)}, f32[16,128,512]{2,1,0:T(8,128)}, u32[]{:S(2)}) %copy-start) | copy-done | bytes 4194328
  2.2 0.0 copy-start.1
  2.2 1.1 %copy-done.1 = bf16[2,512,384]{2,1,0:T(8,128)(2,1)S(1)} copy-done((bf16[2,512,384]{2,1,0:T(8,128)(2,1)S(1)}, bf16[2,512,384]{2,1,0:T(8,128)(2,1)}, u32[]{:S(2)}) %copy-start.1) | copy-done | bytes 786456
  3.3 0.0 copy-start.3
  3.3 1.2 %copy-done.3 = bf16[2,128,2048]{2,1,0:T(8,128)(2,1)S(1)} copy-done((bf16[2,128,2048]{2,1,0:T(8,128)(2,1)S(1)}, bf16[2,128,2048]{2,1,0:T(8,128)(2,1)}, u32[]{:S(2)}) %copy-start.3) | copy-done | bytes 1048600
  4.5 0.0 copy-start.4
  4.5 1.0 %copy-done.4 = f32[512,2,128]{2,1,0:T(2,128)S(1)} copy-done((f32[512,2,128]{2,1,0:T(2,128)S(1)}, f32[512,2,128]{2,1,0:T(2,128)}, u32[]{:S(2)}) %copy-start.4) | copy-done | bytes 524312
  5.6 0.0 copy-start.5
  5.6 1.0 %copy-done.5 = f32[512,2,128]{2,1,0:T(2,128)S(1)} copy-done((f32[512,2,128]{2,1,0:T(2,128)S(1)}, f32[512,2,128]{2,1,0:T(2,128)}, u32[]{:S(2)}) %copy-start.5) | copy-done | bytes 524312
  6.6 0.0 copy-start.6
  6.6 0.7 %copy-done.6 = s32[2,16]{1,0:T(2,128)S(1)} copy-done((s32[2,16]{1,0:T(2,128)S(1)}, s32[2,16]{1,0:T(2,128)}, u32[]{:S(2)}) %copy-start.6) | copy-done | bytes 152
  7.3 0.0 copy-start.7
  7.3 0.7 %copy-done.7 = s32[2,16]{1,0:T(2,128)S(1)} copy-done((s32[2,16]{1,0:T(2,128)S(1)}, s32[2,16]{1,0:T(2,128)}, u32[]{:S(2)}) %copy-start.7) | copy-done | bytes 152
  8.0 0.0 copy-start.2
  8.0 33.7 %project_and_spread.1.spread = bf16[3,2,128,128]{3,2,1,0:T(8,128)(2,1)S(1)} custom-call(s32[2,16]{1,0:T(2,128)S(1)} %copy-done.6, s32[2,16]{1,0:T(2,128)S(1)} %copy-done.7, f32[16,128,512]{2,1,0:T(8,128)S(1)} %copy-done, bf16[2,512,384]{2,1,0:T(8,128)(2,1)S(1)} %copy-done.1, bf16[2,128,2048]{2,1,0:T(8,128)(2,1)S(1)} %copy-done.3, f32[1024,128]{1,0:T(8,128)S(1)} %bitcast.2, ...), custom_call_target="tpu_custom_call" | custom-call | tf_op jit(solution)/shard_map/project_and_spread/pallas_call | solution.py:247
  41.7 0.0 copy-done.2
  41.8 5.1 %backproject.1 = f32[16,128,512]{2,1,0:T(8,128)} custom-call(s32[2,16]{1,0:T(2,128)S(1)} %copy-done.6, s32[2,16]{1,0:T(2,128)S(1)} %copy-done.7, bf16[3,2,128,128]{3,2,1,0:T(8,128)(2,1)S(1)} %project_and_spread.1.spread, bf16[2,512,384]{2,1,0:T(8,128)(2,1)S(1)} %copy-done.1, f32[16,128,512]{2,1,0:T(8,128)S(1)} %copy-done, bf16[16,128,512]{2,1,0:T(8,128)(2,1)S(1)} %copy-done.2), custom_call_target="tpu_custom_call" | custom-call | tf_op jit(solution)/shard_map/backproject/pallas_call | solution.py:322
Async XLA Ops:
  0.0 2.2 %copy-start = (f32[16,128,512]{2,1,0:T(8,128)S(1)}, f32[16,128,512]{2,1,0:T(8,128)}, u32[]{:S(2)}) copy-start(f32[16,128,512]{2,1,0:T(8,128)} %volume.3) | copy-start | bytes 12582916
  2.2 1.1 %copy-start.1 = (bf16[2,512,384]{2,1,0:T(8,128)(2,1)S(1)}, bf16[2,512,384]{2,1,0:T(8,128)(2,1)}, u32[]{:S(2)}) copy-start(bf16[2,512,384]{2,1,0:T(8,128)(2,1)} %depth.3) | copy-start | bytes 2359300
  3.3 1.2 %copy-start.3 = (bf16[2,128,2048]{2,1,0:T(8,128)(2,1)S(1)}, bf16[2,128,2048]{2,1,0:T(8,128)(2,1)}, u32[]{:S(2)}) copy-start(bf16[2,128,2048]{2,1,0:T(8,128)(2,1)} %colmap.1) | copy-start | bytes 3145732
  4.5 1.0 %copy-start.4 = (f32[512,2,128]{2,1,0:T(2,128)S(1)}, f32[512,2,128]{2,1,0:T(2,128)}, u32[]{:S(2)}) copy-start(f32[512,2,128]{2,1,0:T(2,128)} %param.12) | copy-start | bytes 1572868
  5.6 1.0 %copy-start.5 = (f32[512,2,128]{2,1,0:T(2,128)S(1)}, f32[512,2,128]{2,1,0:T(2,128)}, u32[]{:S(2)}) copy-start(f32[512,2,128]{2,1,0:T(2,128)} %param.13) | copy-start | bytes 1572868
  6.6 0.7 %copy-start.6 = (s32[2,16]{1,0:T(2,128)S(1)}, s32[2,16]{1,0:T(2,128)}, u32[]{:S(2)}) copy-start(s32[2,16]{1,0:T(2,128)} %start_ref.3) | copy-start | bytes 388
  7.3 0.7 %copy-start.7 = (s32[2,16]{1,0:T(2,128)S(1)}, s32[2,16]{1,0:T(2,128)}, u32[]{:S(2)}) copy-start(s32[2,16]{1,0:T(2,128)} %len_ref.3) | copy-start | bytes 388
  8.0 33.8 %copy-start.2 = (bf16[16,128,512]{2,1,0:T(8,128)(2,1)S(1)}, bf16[16,128,512]{2,1,0:T(8,128)(2,1)}, u32[]{:S(2)}) copy-start(bf16[16,128,512]{2,1,0:T(8,128)(2,1)} %col_weight.1) | copy-start | bytes 6291460

commit v2 on v1

--- a/solution.py
+++ b/solution.py
@@ -10,6 +10,7 @@
 BLK = 128
 VIEWS = 2
 CHUNK = 4
+GRANT = 64 * 1024 * 1024 - 64 * 1024
 MESH = pl.DeviceIdType.MESH
 BF16 = jnp.bfloat16
 F32 = jnp.float32
@@ -17,9 +18,9 @@
 
 def middle_kernel(
     n, groups,
-    start_ref, len_ref, volume, depth, colmap, measured, weight,
+    starts, lens, volume, depth, colmap, measured, weight,
     out_ref,
-    vol, dcat, maps, meas, rw, meas_t, rw_t, acc, wt, halo, gathered, part, parts_in, own, halo_s,
+    start_ref, len_ref, vol, dcat, maps, meas, rw, meas_t, rw_t, acc, wt, halo, gathered, part, parts_in, own, halo_s,
     vol_sem, dep_sem, loc_sem,
     m_send, m_recv, f_send, f_recv, h_send, h_recv, g_send, g_recv, r_send, r_recv, s_send, s_recv,
 ):
@@ -52,6 +53,12 @@
 
     for k in range(steps):
         vol_copy(k).start()
+    band_copies = [
+        pltpu.make_async_copy(starts, start_ref, loc_sem.at[3]),
+        pltpu.make_async_copy(lens, len_ref, loc_sem.at[4]),
+    ]
+    for copy in band_copies:
+        copy.start()
     local_copies = [
         pltpu.make_async_copy(colmap.at[:, :, my_columns(me)], maps.at[:, x_rows(me), :], loc_sem.at[0]),
         pltpu.make_async_copy(measured, meas, loc_sem.at[1]),
@@ -89,7 +96,7 @@
         map_copy(d).start()
 
     acc[...] = jnp.zeros_like(acc)
-    for copy in depth_copies:
+    for copy in depth_copies + band_copies:
         copy.wait()
 
     def forward(k, carry):
@@ -241,15 +248,16 @@
     views, _, t_len = depth_map.shape
     cols = measured.shape[0]
     hbm = pl.BlockSpec(memory_space=pl.ANY)
-    smem = pl.BlockSpec(memory_space=pltpu.SMEM)
     block = (views, BLK, BLK)
     dma = pltpu.SemaphoreType.DMA
     return pl.pallas_call(
         functools.partial(middle_kernel, n, groups),
         out_shape=jax.ShapeDtypeStruct((3, *block), BF16),
-        in_specs=[smem, smem, hbm, hbm, hbm, hbm, hbm],
+        in_specs=[hbm] * 7,
         out_specs=pl.BlockSpec(memory_space=pltpu.VMEM),
         scratch_shapes=[
+            pltpu.SMEM((views, slices), jnp.int32),
+            pltpu.SMEM((views, slices), jnp.int32),
             pltpu.VMEM((slices, x_columns, y_cells), F32),
             pltpu.VMEM((y_cells, views * t_len), BF16),
             pltpu.VMEM((views, n * BLK, cols), BF16),
@@ -265,12 +273,12 @@
             pltpu.VMEM((n, *block), BF16),
             pltpu.VMEM((n, *block), F32),
             pltpu.VMEM((3, *block), BF16),
-            dma((slices // CHUNK,)), dma((views,)), dma((3,)),
+            dma((slices // CHUNK,)), dma((views,)), dma((5,)),
             dma((n,)), dma((n,)), dma((n,)), dma((n,)), dma((2,)), dma((2,)),
             dma((n,)), dma((n,)), dma((n,)), dma((n,)), dma((2,)), dma((2,)),
         ],
         compiler_params=pltpu.CompilerParams(
-            collective_id=0, has_side_effects=True, vmem_limit_bytes=32 * 1024 * 1024
+            collective_id=0, has_side_effects=True, vmem_limit_bytes=GRANT
         ),
         name="project_and_spread",
     )(
@@ -279,59 +287,97 @@
     )
 
 
-def back_kernel(start_ref, len_ref, spread, depth, volume, col_weight, out_ref, images):
+def back_kernel(
+    starts, lens, spread_in, depth_in, volume, col_weight, out,
+    start_ref, len_ref, spread, depth, vol, cw, images, result,
+    in_sem, vol_sem, cw_sem, out_sem,
+):
     g = lax.axis_index("gz")
-    step = pl.program_id(0)
+    slices = vol.shape[0]
+    first_copies = [
+        pltpu.make_async_copy(spread_in, spread, in_sem.at[0]),
+        pltpu.make_async_copy(depth_in, depth, in_sem.at[1]),
+        pltpu.make_async_copy(starts, start_ref, in_sem.at[2]),
+        pltpu.make_async_copy(lens, len_ref, in_sem.at[3]),
+    ]
+    for copy in first_copies:
+        copy.start()
+
+    def part(ref, k):
+        return ref.at[pl.ds(k * CHUNK, CHUNK)]
+
+    def vol_copy(k):
+        return pltpu.make_async_copy(part(volume, k), part(vol, k), vol_sem.at[k])
+
+    def cw_copy(k):
+        return pltpu.make_async_copy(part(col_weight, k), part(cw, k), cw_sem.at[k])
+
+    for k in range(slices // CHUNK):
+        vol_copy(k).start()
+        cw_copy(k).start()
+    for copy in first_copies:
+        copy.wait()
     depth_contract = (((1,), (1,)), ((), ()))
-
-    @pl.when(step == 0)
-    def _():
-        for v in range(VIEWS):
-            low = jnp.concatenate([spread[0, v], spread[1, v]], axis=1)
-            high = jnp.concatenate([spread[1, v], spread[2, v]], axis=1)
-            pair = lax.dot_general(
-                jnp.concatenate([low, high], axis=0), depth[v, :, :2 * BLK],
-                depth_contract, preferred_element_type=F32,
-            )
-            images[v, 0] = lax.dot_general(
-                spread[1, v], depth[v, :, :BLK], depth_contract, preferred_element_type=F32
-            )
-            images[v, 1] = pair[:BLK]
-            images[v, 2] = pair[BLK:]
-            images[v, 3] = pair[:BLK] + lax.dot_general(
-                spread[2, v], depth[v, :, 2 * BLK:], depth_contract, preferred_element_type=F32
-            )
-
-    count = volume.shape[0]
-    for i in range(count):
-        z = step * count + i
-        total = None
-        for v in range(VIEWS):
-            low = (start_ref[v, z] < g * BLK).astype(jnp.int32)
-            up = (start_ref[v, z] + len_ref[v, z] > (g + 1) * BLK).astype(jnp.int32)
-            image = images[v, low + 2 * up]
-            total = image if total is None else total + image
-        out_ref[i] = volume[i] + col_weight[i].astype(F32) * total
+    for v in range(VIEWS):
+        low = jnp.concatenate([spread[0, v], spread[1, v]], axis=1)
+        high = jnp.concatenate([spread[1, v], spread[2, v]], axis=1)
+        pair = lax.dot_general(
+            jnp.concatenate([low, high], axis=0), depth[v, :, :2 * BLK],
+            depth_contract, preferred_element_type=F32,
+        )
+        images[v, 0] = lax.dot_general(
+            spread[1, v], depth[v, :, :BLK], depth_contract, preferred_element_type=F32
+        )
+        images[v, 1] = pair[:BLK]
+        images[v, 2] = pair[BLK:]
+        images[v, 3] = pair[:BLK] + lax.dot_general(
+            spread[2, v], depth[v, :, 2 * BLK:], depth_contract, preferred_element_type=F32
+        )
+
+    def out_copy(z):
+        return pltpu.make_async_copy(result.at[z], out.at[z], out_sem.at[z])
+
+    def update(k, carry):
+        vol_copy(k).wait()
+        cw_copy(k).wait()
+        for i in range(CHUNK):
+            z = k * CHUNK + i
+            total = None
+            for v in range(VIEWS):
+                low = (start_ref[v, z] < g * BLK).astype(jnp.int32)
+                up = (start_ref[v, z] + len_ref[v, z] > (g + 1) * BLK).astype(jnp.int32)
+                image = images[v, low + 2 * up]
+                total = image if total is None else total + image
+            result[z] = vol[z] + cw[z].astype(F32) * total
+            out_copy(z).start()
+        return carry
+
+    lax.fori_loop(0, slices // CHUNK, update, 0)
+    for z in range(slices):
+        out_copy(z).wait()
 
 
 def back(spread, depth_map, volume, col_weight, band_start, band_len):
     slices, x_columns, y_cells = volume.shape
-    count = 2
-    smem = pl.BlockSpec(memory_space=pltpu.SMEM)
-    slab = pl.BlockSpec((count, x_columns, y_cells), lambda i: (i, 0, 0))
+    hbm = pl.BlockSpec(memory_space=pl.ANY)
+    dma = pltpu.SemaphoreType.DMA
     return pl.pallas_call(
         back_kernel,
-        grid=(slices // count,),
         out_shape=jax.ShapeDtypeStruct(volume.shape, F32),
-        in_specs=[
-            smem, smem,
-            pl.BlockSpec(spread.shape, lambda i: (0, 0, 0, 0)),
-            pl.BlockSpec(depth_map.shape, lambda i: (0, 0, 0)),
-            slab, slab,
+        in_specs=[hbm] * 6,
+        out_specs=hbm,
+        scratch_shapes=[
+            pltpu.SMEM(band_start.shape, jnp.int32),
+            pltpu.SMEM(band_start.shape, jnp.int32),
+            pltpu.VMEM(spread.shape, BF16),
+            pltpu.VMEM(depth_map.shape, BF16),
+            pltpu.VMEM(volume.shape, F32),
+            pltpu.VMEM(volume.shape, BF16),
+            pltpu.VMEM((VIEWS, 4, x_columns, y_cells), F32),
+            pltpu.VMEM(volume.shape, F32),
+            dma((4,)), dma((slices // CHUNK,)), dma((slices // CHUNK,)), dma((slices,)),
         ],
-        out_specs=slab,
-        scratch_shapes=[pltpu.VMEM((VIEWS, 4, x_columns, y_cells), F32)],
-        compiler_params=pltpu.CompilerParams(vmem_limit_bytes=32 * 1024 * 1024),
+        compiler_params=pltpu.CompilerParams(vmem_limit_bytes=GRANT),
         name="backproject",
     )(band_start, band_len, spread, depth_map, volume, col_weight)
 

time: 47.2 us -> 38.3 us (0.81)
  local copies, waits for them, and re-layouts: 7.99 us -> 0 us
  Pallas kernels: 38.9 us -> 38.2 us
    unnamed x16 -> x0, local copies, waits for them, and re-layouts: 7.99 us -> none
    pallas_call x1, Pallas kernels: 5.11 us -> 4.55 us  [back(): pl.pallas_call(back_kernel, out_shape=jax.ShapeDtypeStruct(volume.shape,...]
where the time goes in v2:
time: 38.3 us; the launch traced here: 38.2 us
  Pallas kernels  38.2 us (100%)
    pallas_call x1, Pallas kernels, middle(): pl.pallas_call(functools.partial(middle_kernel, n, groups), out_shape=jax...  33.6 us
    pallas_call x1, Pallas kernels, back(): pl.pallas_call(back_kernel, out_shape=jax.ShapeDtypeStruct(volume.shape,...  4.55 us

profile of v2, /device:TPU:1, one launch (start us, length us, event | category | flops | bytes accessed | tf_op | source)
XLA Modules:
  0.0 38.2 jit_solution(6592842017669645547)
XLA Ops:
  0.0 33.6 %project_and_spread.1.spread_in = bf16[3,2,128,128]{3,2,1,0:T(8,128)(2,1)} custom-call(s32[2,16]{1,0:T(2,128)} %starts.3, s32[2,16]{1,0:T(2,128)} %lens.3, f32[16,128,512]{2,1,0:T(8,128)} %volume.3, bf16[2,512,384]{2,1,0:T(8,128)(2,1)} %depth_in.1, bf16[2,128,2048]{2,1,0:T(8,128)(2,1)} %colmap.1, f32[1024,128]{1,0:T(8,128)} %bitcast.2, f32[1024,128]{1,0:T(8,128)} %bitcast.3), custom_call_target="tpu_custom_call" | custom-call | tf_op jit(solution)/shard_map/project_and_spread/pallas_call | solution.py:253
  33.6 4.6 %backproject.1 = f32[16,128,512]{2,1,0:T(8,128)} custom-call(s32[2,16]{1,0:T(2,128)} %starts.3, s32[2,16]{1,0:T(2,128)} %lens.3, bf16[3,2,128,128]{3,2,1,0:T(8,128)(2,1)} %project_and_spread.1.spread_in, bf16[2,512,384]{2,1,0:T(8,128)(2,1)} %depth_in.1, f32[16,128,512]{2,1,0:T(8,128)} %volume.3, bf16[16,128,512]{2,1,0:T(8,128)(2,1)} %col_weight.1), custom_call_target="tpu_custom_call" | custom-call | tf_op jit(solution)/shard_map/backproject/pallas_call | solution.py:364

commit v3 on v2

--- a/solution.py
+++ b/solution.py
@@ -22,12 +22,15 @@
     out_ref,
     start_ref, len_ref, vol, dcat, maps, meas, rw, meas_t, rw_t, acc, wt, halo, gathered, part, parts_in, own, halo_s,
     vol_sem, dep_sem, loc_sem,
-    m_send, m_recv, f_send, f_recv, h_send, h_recv, g_send, g_recv, r_send, r_recv, s_send, s_recv,
+    m_send, m_recv, x_send, x_recv, f_send, f_recv, h_send, h_recv, g_send, g_recv, r_send, r_recv, s_send, s_recv,
 ):
     g = lax.axis_index("gz")
     me = lax.axis_index("gx")
     core = lax.rem(g, 2)
     sibling = g + 1 - 2 * core
+    half = lax.rem(g // 2, 2)
+    across = g + 2 - 4 * half
+    rows = BLK // 2
     cols = maps.shape[2]
     slices = vol.shape[0]
     steps = slices // CHUNK
@@ -79,17 +82,37 @@
     def _():
         pl.semaphore_signal(barrier, inc=1, device_id={"gz": g + 1}, device_id_type=MESH)
 
+    pl.semaphore_signal(barrier, inc=1, device_id={"gz": across}, device_id_type=MESH)
     below = jnp.where(g > 0, 1, 0)
     above = jnp.where(g < groups - 1, 1, 0)
-    pl.semaphore_wait(barrier, n - 1 + below + above)
+    pl.semaphore_wait(barrier, n + below + above)
+
+    def piece(view, who, which):
+        return maps.at[view, pl.ds(pl.multiple_of(who * BLK + which * rows, rows), rows), :]
 
     def map_copy(d):
         peer = lax.rem(me + d, n)
         return pltpu.make_async_remote_copy(
-            src_ref=colmap.at[core, :, my_columns(peer)],
-            dst_ref=maps.at[core, x_rows(me), :],
+            src_ref=colmap.at[core, pl.ds(pl.multiple_of(half * rows, rows), rows), my_columns(peer)],
+            dst_ref=piece(core, me, half),
             send_sem=m_send.at[d], recv_sem=m_recv.at[d],
             device_id={"gx": peer}, device_id_type=MESH,
+        )
+
+    def across_copy(d, which):
+        src = piece(core, lax.rem(me - d + n, n), which)
+        return pltpu.make_async_remote_copy(
+            src_ref=src, dst_ref=src,
+            send_sem=x_send.at[d], recv_sem=x_recv.at[d],
+            device_id={"gz": across}, device_id_type=MESH,
+        )
+
+    def forward_copy(d, view, came, which):
+        src = piece(view, lax.rem(me - d + n, n), which)
+        return pltpu.make_async_remote_copy(
+            src_ref=src, dst_ref=src,
+            send_sem=f_send.at[came, d], recv_sem=f_recv.at[came, d],
+            device_id={"gz": sibling}, device_id_type=MESH,
         )
 
     for d in range(1, n):
@@ -125,86 +148,92 @@
         for v in range(VIEWS):
             wt[b // 2, v] = acc[v, b].T.astype(BF16)
 
-    def to_below(src, dst, send, recv):
-        return pltpu.make_async_remote_copy(
-            src_ref=src, dst_ref=dst, send_sem=send.at[0], recv_sem=recv.at[0],
+    def to_below(src, land, send, recv, v):
+        return pltpu.make_async_remote_copy(
+            src_ref=src, dst_ref=land.at[1, v], send_sem=send.at[0, v], recv_sem=recv.at[0, v],
             device_id={"gz": g - 1}, device_id_type=MESH,
         )
 
-    def to_above(src, dst, send, recv):
-        return pltpu.make_async_remote_copy(
-            src_ref=src, dst_ref=dst, send_sem=send.at[1], recv_sem=recv.at[1],
+    def to_above(src, land, send, recv, v):
+        return pltpu.make_async_remote_copy(
+            src_ref=src, dst_ref=land.at[0, v], send_sem=send.at[1, v], recv_sem=recv.at[1, v],
             device_id={"gz": g + 1}, device_id_type=MESH,
         )
 
-    def exchange_start(low_src, high_src, land, send, recv):
+    def exchange_start(low_src, high_src, land, send, recv, v):
         @pl.when(g > 0)
         def _():
-            to_below(low_src, land.at[1], send, recv).start()
+            to_below(low_src, land, send, recv, v).start()
 
         @pl.when(g < groups - 1)
         def _():
-            to_above(high_src, land.at[0], send, recv).start()
+            to_above(high_src, land, send, recv, v).start()
 
         @pl.when(g == 0)
         def _():
-            land[0] = jnp.zeros_like(land[0])
+            land[0, v] = jnp.zeros_like(land[0, v])
 
         @pl.when(g == groups - 1)
         def _():
-            land[1] = jnp.zeros_like(land[1])
-
-    def exchange_wait(low_src, high_src, land, send, recv):
+            land[1, v] = jnp.zeros_like(land[1, v])
+
+    def exchange_wait(low_src, high_src, land, send, recv, v):
         @pl.when(g > 0)
         def _():
-            to_below(low_src, land.at[1], send, recv).wait_send()
-            to_above(high_src, land.at[0], send, recv).wait_recv()
+            to_below(low_src, land, send, recv, v).wait_send()
+            to_above(high_src, land, send, recv, v).wait_recv()
 
         @pl.when(g < groups - 1)
         def _():
-            to_above(high_src, land.at[0], send, recv).wait_send()
-            to_below(low_src, land.at[1], send, recv).wait_recv()
-
-    exchange_start(wt.at[0], wt.at[1], halo, h_send, h_recv)
+            to_above(high_src, land, send, recv, v).wait_send()
+            to_below(low_src, land, send, recv, v).wait_recv()
+
+    for v in range(VIEWS):
+        exchange_start(wt.at[0, v], wt.at[1, v], halo, h_send, h_recv, v)
+    for d in range(1, n):
+        map_copy(d).wait_recv()
+        across_copy(d, half).start()
+        forward_copy(d, core, 0, half).start()
     for copy in local_copies:
         copy.wait()
     for v in range(VIEWS):
         meas_t[v] = meas[pl.ds(v, cols, stride=VIEWS), :].T
         rw_t[v] = rw[pl.ds(v, cols, stride=VIEWS), :].T
     middle = [acc[v, 1].T.astype(BF16).astype(F32) for v in range(VIEWS)]
-    exchange_wait(wt.at[0], wt.at[1], halo, h_send, h_recv)
-    for v in range(VIEWS):
+    for v in range(VIEWS):
+        exchange_wait(wt.at[0, v], wt.at[1, v], halo, h_send, h_recv, v)
         total = middle[v] + halo[0, v].astype(F32) + halo[1, v].astype(F32)
         gathered[me, v] = total.astype(BF16)
 
-    def gather_copy(d, slot):
-        return pltpu.make_async_remote_copy(
-            src_ref=gathered.at[slot], dst_ref=gathered.at[slot],
-            send_sem=g_send.at[d], recv_sem=g_recv.at[d],
+    def gather_copy(d, v, slot):
+        return pltpu.make_async_remote_copy(
+            src_ref=gathered.at[slot, v], dst_ref=gathered.at[slot, v],
+            send_sem=g_send.at[v, d], recv_sem=g_recv.at[v, d],
             device_id={"gx": lax.rem(me + d, n)}, device_id_type=MESH,
         )
 
+    for v in range(VIEWS):
+        for d in range(1, n):
+            gather_copy(d, v, me).start()
     for d in range(1, n):
-        gather_copy(d, me).start()
-
-    def forward_copy(d, view):
-        src = lax.rem(me - d + n, n)
-        return pltpu.make_async_remote_copy(
-            src_ref=maps.at[view, x_rows(src), :], dst_ref=maps.at[view, x_rows(src), :],
-            send_sem=f_send.at[d], recv_sem=f_recv.at[d],
-            device_id={"gz": sibling}, device_id_type=MESH,
-        )
-
-    for d in range(1, n):
-        map_copy(d).wait_recv()
-        forward_copy(d, core).start()
-    for d in range(1, n):
-        gather_copy(d, lax.rem(me - d + n, n)).wait_recv()
-    for d in range(1, n):
-        forward_copy(d, 1 - core).wait_recv()
-
-    own_parts = []
-    for v in range(VIEWS):
+        across_copy(d, 1 - half).wait_recv()
+        forward_copy(d, core, 1, 1 - half).start()
+
+    def reduce_copy(d, v):
+        peer = lax.rem(me + d, n)
+        return pltpu.make_async_remote_copy(
+            src_ref=part.at[peer, v], dst_ref=parts_in.at[d, v],
+            send_sem=r_send.at[v, d], recv_sem=r_recv.at[v, d],
+            device_id={"gx": peer}, device_id_type=MESH,
+        )
+
+    for v in range(VIEWS):
+        if v == 0:
+            for d in range(1, n):
+                forward_copy(d, 1 - core, 0, half).wait_recv()
+                forward_copy(d, 1 - core, 1, 1 - half).wait_recv()
+        for d in range(1, n):
+            gather_copy(d, v, lax.rem(me - d + n, n)).wait_recv()
         window = jnp.concatenate([gathered[j, v] for j in range(n)], axis=1)
         projection = jnp.dot(window, maps[v], preferred_element_type=F32)
         residual = (rw_t[v] * (meas_t[v] - projection)).astype(BF16)
@@ -212,34 +241,30 @@
         for j in range(n):
             own[j, v] = spread[:, j * BLK:(j + 1) * BLK]
             part[j, v] = spread[:, j * BLK:(j + 1) * BLK].astype(BF16)
-
-    def reduce_copy(d):
-        peer = lax.rem(me + d, n)
-        return pltpu.make_async_remote_copy(
-            src_ref=part.at[peer], dst_ref=parts_in.at[d],
-            send_sem=r_send.at[d], recv_sem=r_recv.at[d],
-            device_id={"gx": peer}, device_id_type=MESH,
-        )
-
-    for d in range(1, n):
-        reduce_copy(d).start()
-    totals = [own[me, v] for v in range(VIEWS)]
-    for d in range(1, n):
-        reduce_copy(d).wait_recv()
-        totals = [totals[v] + parts_in[d, v].astype(F32) for v in range(VIEWS)]
-    for v in range(VIEWS):
-        halo_s[2, v] = totals[v].T.astype(BF16)
-
-    exchange_start(halo_s.at[2], halo_s.at[2], halo_s, s_send, s_recv)
+        for d in range(1, n):
+            reduce_copy(d, v).start()
+
+    for v in range(VIEWS):
+        total = own[me, v]
+        for d in range(1, n):
+            reduce_copy(d, v).wait_recv()
+            total = total + parts_in[d, v].astype(F32)
+        halo_s[2, v] = total.T.astype(BF16)
+        exchange_start(halo_s.at[2, v], halo_s.at[2, v], halo_s, s_send, s_recv, v)
+
     out_ref[1] = halo_s[2]
-    exchange_wait(halo_s.at[2], halo_s.at[2], halo_s, s_send, s_recv)
+    for v in range(VIEWS):
+        exchange_wait(halo_s.at[2, v], halo_s.at[2, v], halo_s, s_send, s_recv, v)
     out_ref[0] = halo_s[0]
     out_ref[2] = halo_s[1]
     for d in range(1, n):
         map_copy(d).wait_send()
-        gather_copy(d, me).wait_send()
-        forward_copy(d, core).wait_send()
-        reduce_copy(d).wait_send()
+        across_copy(d, half).wait_send()
+        forward_copy(d, core, 0, half).wait_send()
+        forward_copy(d, core, 1, 1 - half).wait_send()
+        for v in range(VIEWS):
+            gather_copy(d, v, me).wait_send()
+            reduce_copy(d, v).wait_send()
 
 
 def middle(volume, column_map, depth_map, measured, row_weight, band_start, band_len):
@@ -274,8 +299,9 @@
             pltpu.VMEM((n, *block), F32),
             pltpu.VMEM((3, *block), BF16),
             dma((slices // CHUNK,)), dma((views,)), dma((5,)),
-            dma((n,)), dma((n,)), dma((n,)), dma((n,)), dma((2,)), dma((2,)),
-            dma((n,)), dma((n,)), dma((n,)), dma((n,)), dma((2,)), dma((2,)),
+            dma((n,)), dma((n,)), dma((n,)), dma((n,)), dma((2, n)), dma((2, n)),
+            dma((2, views)), dma((2, views)), dma((views, n)), dma((views, n)),
+            dma((views, n)), dma((views, n)), dma((2, views)), dma((2, views)),
         ],
         compiler_params=pltpu.CompilerParams(
             collective_id=0, has_side_effects=True, vmem_limit_bytes=GRANT

time: 38.3 us -> 33.4 us (0.87)
  Pallas kernels: 38.2 us -> 33.3 us
    pallas_call x1, Pallas kernels: 33.6 us -> 28.7 us  [middle(): pl.pallas_call(functools.partial(middle_kernel, n, groups), out_shape=jax...]
where the time goes in v3:
time: 33.4 us; the launch traced here: 33.3 us
  Pallas kernels  33.3 us (100%)
    pallas_call x1, Pallas kernels, middle(): pl.pallas_call(functools.partial(middle_kernel, n, groups), out_shape=jax...  28.7 us
    pallas_call x1, Pallas kernels, back(): pl.pallas_call(back_kernel, out_shape=jax.ShapeDtypeStruct(volume.shape,...  4.56 us

profile of v3, /device:TPU:1, one launch (start us, length us, event | category | flops | bytes accessed | tf_op | source)
XLA Modules:
  0.0 33.3 jit_solution(10541075795293944779)
XLA Ops:
  0.0 28.7 %project_and_spread.1.spread_in = bf16[3,2,128,128]{3,2,1,0:T(8,128)(2,1)} custom-call(s32[2,16]{1,0:T(2,128)} %starts.3, s32[2,16]{1,0:T(2,128)} %lens.3, f32[16,128,512]{2,1,0:T(8,128)} %volume.3, bf16[2,512,384]{2,1,0:T(8,128)(2,1)} %depth_in.1, bf16[2,128,2048]{2,1,0:T(8,128)(2,1)} %colmap.1, f32[1024,128]{1,0:T(8,128)} %bitcast.2, f32[1024,128]{1,0:T(8,128)} %bitcast.3), custom_call_target="tpu_custom_call" | custom-call | tf_op jit(solution)/shard_map/project_and_spread/pallas_call | solution.py:278
  28.7 4.6 %backproject.1 = f32[16,128,512]{2,1,0:T(8,128)} custom-call(s32[2,16]{1,0:T(2,128)} %starts.3, s32[2,16]{1,0:T(2,128)} %lens.3, bf16[3,2,128,128]{3,2,1,0:T(8,128)(2,1)} %project_and_spread.1.spread_in, bf16[2,512,384]{2,1,0:T(8,128)(2,1)} %depth_in.1, f32[16,128,512]{2,1,0:T(8,128)} %volume.3, bf16[16,128,512]{2,1,0:T(8,128)(2,1)} %col_weight.1), custom_call_target="tpu_custom_call" | custom-call | tf_op jit(solution)/shard_map/backproject/pallas_call | solution.py:390

commit v4 on v3

--- a/solution.py
+++ b/solution.py
@@ -20,9 +20,9 @@
     n, groups,
     starts, lens, volume, depth, colmap, measured, weight,
     out_ref,
-    start_ref, len_ref, vol, dcat, maps, meas, rw, meas_t, rw_t, acc, wt, halo, gathered, part, parts_in, own, halo_s,
+    start_ref, len_ref, vol, dcat, maps, meas, rw, meas_t, rw_t, acc, wt, halo, gathered, part, parts_in, own, halo_s, extra,
     vol_sem, dep_sem, loc_sem,
-    m_send, m_recv, x_send, x_recv, f_send, f_recv, h_send, h_recv, g_send, g_recv, r_send, r_recv, s_send, s_recv,
+    m_send, m_recv, x_send, x_recv, f_send, f_recv, h_send, h_recv, g_send, g_recv, r_send, r_recv, s_send, s_recv, relay_send, e_send, e_recv,
 ):
     g = lax.axis_index("gz")
     me = lax.axis_index("gx")
@@ -118,103 +118,114 @@
     for d in range(1, n):
         map_copy(d).start()
 
+    def to_below(src, land, send, recv, v):
+        return pltpu.make_async_remote_copy(
+            src_ref=src, dst_ref=land.at[1, v], send_sem=send.at[0, v], recv_sem=recv.at[0, v],
+            device_id={"gz": g - 1}, device_id_type=MESH,
+        )
+
+    def to_above(src, land, send, recv, v):
+        return pltpu.make_async_remote_copy(
+            src_ref=src, dst_ref=land.at[0, v], send_sem=send.at[1, v], recv_sem=recv.at[1, v],
+            device_id={"gz": g + 1}, device_id_type=MESH,
+        )
+
+    def exchange_start(low_src, high_src, land, send, recv, v):
+        @pl.when(g > 0)
+        def _():
+            to_below(low_src, land, send, recv, v).start()
+
+        @pl.when(g < groups - 1)
+        def _():
+            to_above(high_src, land, send, recv, v).start()
+
+        @pl.when(g == 0)
+        def _():
+            land[0, v] = jnp.zeros_like(land[0, v])
+
+        @pl.when(g == groups - 1)
+        def _():
+            land[1, v] = jnp.zeros_like(land[1, v])
+
+    def exchange_wait(low_src, high_src, land, send, recv, v):
+        @pl.when(g > 0)
+        def _():
+            to_below(low_src, land, send, recv, v).wait_send()
+            to_above(high_src, land, send, recv, v).wait_recv()
+
+        @pl.when(g < groups - 1)
+        def _():
+            to_above(high_src, land, send, recv, v).wait_send()
+            to_below(low_src, land, send, recv, v).wait_recv()
+
+    def gather_copy(d, v, slot):
+        return pltpu.make_async_remote_copy(
+            src_ref=gathered.at[slot, v], dst_ref=gathered.at[slot, v],
+            send_sem=g_send.at[v, d], recv_sem=g_recv.at[v, d],
+            device_id={"gx": lax.rem(me + d, n)}, device_id_type=MESH,
+        )
+
+    def relay_copy(v, end, other):
+        return pltpu.make_async_remote_copy(
+            src_ref=gathered.at[other, v], dst_ref=gathered.at[other, v],
+            send_sem=relay_send.at[v], recv_sem=g_recv.at[v, (end - other) % n],
+            device_id={"gx": end}, device_id_type=MESH,
+        )
+
+    def each_sent(do, v):
+        for d in range(1, n):
+            if d == n - 1:
+                pl.when(me != 0)(functools.partial(do, d, v))
+            elif d == 1:
+                pl.when(me != n - 1)(functools.partial(do, d, v))
+            else:
+                do(d, v)
+
     acc[...] = jnp.zeros_like(acc)
     for copy in depth_copies + band_copies:
         copy.wait()
 
-    def forward(k, carry):
-        vol_copy(k).wait()
+    def forward(v, k, carry):
+        if v == 0:
+            vol_copy(k).wait()
         coarse = vol[pl.ds(k * CHUNK, CHUNK)].astype(BF16).reshape(CHUNK * BLK, vol.shape[2])
-        foot = jnp.dot(coarse, dcat[...], preferred_element_type=F32)
-        for v in range(VIEWS):
-            sums = [acc[v, b] for b in range(3)]
-            for i in range(CHUNK):
-                z = k * CHUNK + i
-                low = jnp.where(start_ref[v, z] < g * BLK, 1.0, 0.0).astype(F32)
-                up = jnp.where(start_ref[v, z] + len_ref[v, z] > (g + 1) * BLK, 1.0, 0.0).astype(F32)
-                t = [
-                    foot[i * BLK:(i + 1) * BLK, v * t_len + b * BLK:v * t_len + (b + 1) * BLK]
-                    for b in range(3)
-                ]
-                sums[0] = sums[0] + low * t[0]
-                sums[1] = sums[1] + low * t[1] + (1.0 - low) * t[0]
-                sums[2] = sums[2] + (low * up) * t[2] + ((1.0 - low) * up) * t[1]
-            for b in range(3):
-                acc[v, b] = sums[b]
+        foot = jnp.dot(coarse, dcat[:, v * t_len:(v + 1) * t_len], preferred_element_type=F32)
+        sums = [acc[v, b] for b in range(3)]
+        for i in range(CHUNK):
+            z = k * CHUNK + i
+            low = jnp.where(start_ref[v, z] < g * BLK, 1.0, 0.0).astype(F32)
+            up = jnp.where(start_ref[v, z] + len_ref[v, z] > (g + 1) * BLK, 1.0, 0.0).astype(F32)
+            t = [foot[i * BLK:(i + 1) * BLK, b * BLK:(b + 1) * BLK] for b in range(3)]
+            sums[0] = sums[0] + low * t[0]
+            sums[1] = sums[1] + low * t[1] + (1.0 - low) * t[0]
+            sums[2] = sums[2] + (low * up) * t[2] + ((1.0 - low) * up) * t[1]
+        for b in range(3):
+            acc[v, b] = sums[b]
         return carry
 
-    lax.fori_loop(0, steps, forward, 0)
-    for b in (0, 2):
-        for v in range(VIEWS):
+    for v in range(VIEWS):
+        lax.fori_loop(0, steps, functools.partial(forward, v), 0)
+        for b in (0, 2):
             wt[b // 2, v] = acc[v, b].T.astype(BF16)
-
-    def to_below(src, land, send, recv, v):
-        return pltpu.make_async_remote_copy(
-            src_ref=src, dst_ref=land.at[1, v], send_sem=send.at[0, v], recv_sem=recv.at[0, v],
-            device_id={"gz": g - 1}, device_id_type=MESH,
-        )
-
-    def to_above(src, land, send, recv, v):
-        return pltpu.make_async_remote_copy(
-            src_ref=src, dst_ref=land.at[0, v], send_sem=send.at[1, v], recv_sem=recv.at[1, v],
-            device_id={"gz": g + 1}, device_id_type=MESH,
-        )
-
-    def exchange_start(low_src, high_src, land, send, recv, v):
-        @pl.when(g > 0)
-        def _():
-            to_below(low_src, land, send, recv, v).start()
-
-        @pl.when(g < groups - 1)
-        def _():
-            to_above(high_src, land, send, recv, v).start()
-
-        @pl.when(g == 0)
-        def _():
-            land[0, v] = jnp.zeros_like(land[0, v])
-
-        @pl.when(g == groups - 1)
-        def _():
-            land[1, v] = jnp.zeros_like(land[1, v])
-
-    def exchange_wait(low_src, high_src, land, send, recv, v):
-        @pl.when(g > 0)
-        def _():
-            to_below(low_src, land, send, recv, v).wait_send()
-            to_above(high_src, land, send, recv, v).wait_recv()
-
-        @pl.when(g < groups - 1)
-        def _():
-            to_above(high_src, land, send, recv, v).wait_send()
-            to_below(low_src, land, send, recv, v).wait_recv()
-
-    for v in range(VIEWS):
         exchange_start(wt.at[0, v], wt.at[1, v], halo, h_send, h_recv, v)
+
+    def send_window(v):
+        window = acc[v, 1].T.astype(BF16).astype(F32)
+        exchange_wait(wt.at[0, v], wt.at[1, v], halo, h_send, h_recv, v)
+        gathered[me, v] = (window + halo[0, v].astype(F32) + halo[1, v].astype(F32)).astype(BF16)
+        each_sent(lambda d, v: gather_copy(d, v, me).start(), v)
+
+    send_window(0)
     for d in range(1, n):
         map_copy(d).wait_recv()
         across_copy(d, half).start()
         forward_copy(d, core, 0, half).start()
+    send_window(1)
     for copy in local_copies:
         copy.wait()
     for v in range(VIEWS):
         meas_t[v] = meas[pl.ds(v, cols, stride=VIEWS), :].T
         rw_t[v] = rw[pl.ds(v, cols, stride=VIEWS), :].T
-    middle = [acc[v, 1].T.astype(BF16).astype(F32) for v in range(VIEWS)]
-    for v in range(VIEWS):
-        exchange_wait(wt.at[0, v], wt.at[1, v], halo, h_send, h_recv, v)
-        total = middle[v] + halo[0, v].astype(F32) + halo[1, v].astype(F32)
-        gathered[me, v] = total.astype(BF16)
-
-    def gather_copy(d, v, slot):
-        return pltpu.make_async_remote_copy(
-            src_ref=gathered.at[slot, v], dst_ref=gathered.at[slot, v],
-            send_sem=g_send.at[v, d], recv_sem=g_recv.at[v, d],
-            device_id={"gx": lax.rem(me + d, n)}, device_id_type=MESH,
-        )
-
-    for v in range(VIEWS):
-        for d in range(1, n):
-            gather_copy(d, v, me).start()
     for d in range(1, n):
         across_copy(d, 1 - half).wait_recv()
         forward_copy(d, core, 1, 1 - half).start()
@@ -227,13 +238,45 @@
             device_id={"gx": peer}, device_id_type=MESH,
         )
 
-    for v in range(VIEWS):
+    def extra_copy(v, target, neighbour):
+        return pltpu.make_async_remote_copy(
+            src_ref=part.at[target, v], dst_ref=extra.at[v],
+            send_sem=e_send.at[v], recv_sem=e_recv.at[v],
+            device_id={"gx": neighbour}, device_id_type=MESH,
+        )
+
+    def start_reduce(d, v):
+        if d == n - 2 and d == 2:
+            pl.when(jnp.logical_and(me != 1, me != n - 2))(lambda: reduce_copy(d, v).start())
+        elif d == n - 2:
+            pl.when(me != 1)(lambda: reduce_copy(d, v).start())
+        elif d == 2:
+            pl.when(me != n - 2)(lambda: reduce_copy(d, v).start())
+        else:
+            reduce_copy(d, v).start()
+
+    def combine(v):
+        for device, target, d in ((1, n - 1, n - 2), (n - 2, 0, 2)):
+            @pl.when(me == device)
+            def _():
+                extra_copy(v, target, 0).wait_recv()
+                part[target, v] = (own[target, v] + extra[v].astype(F32)).astype(BF16)
+                reduce_copy(d, v).start()
+
+    for v in range(VIEWS):
+        first = sorted({2, n - 2})
+        for d in first + [d for d in range(1, n) if d not in first]:
+            gather_copy(d, v, lax.rem(me - d + n, n)).wait_recv()
+            if d == 2:
+                pl.when(me == 1)(lambda: relay_copy(v, 0, n - 1).start())
+            if d == n - 2:
+                pl.when(me == n - 2)(lambda: relay_copy(v, n - 1, 0).start())
         if v == 0:
             for d in range(1, n):
                 forward_copy(d, 1 - core, 0, half).wait_recv()
                 forward_copy(d, 1 - core, 1, 1 - half).wait_recv()
-        for d in range(1, n):
-            gather_copy(d, v, lax.rem(me - d + n, n)).wait_recv()
+        else:
+            combine(v - 1)
         window = jnp.concatenate([gathered[j, v] for j in range(n)], axis=1)
         projection = jnp.dot(window, maps[v], preferred_element_type=F32)
         residual = (rw_t[v] * (meas_t[v] - projection)).astype(BF16)
@@ -241,13 +284,26 @@
         for j in range(n):
             own[j, v] = spread[:, j * BLK:(j + 1) * BLK]
             part[j, v] = spread[:, j * BLK:(j + 1) * BLK].astype(BF16)
-        for d in range(1, n):
-            reduce_copy(d, v).start()
-
+        pl.when(me == 0)(lambda: extra_copy(v, n - 1, 1).start())
+        pl.when(me == n - 1)(lambda: extra_copy(v, 0, n - 2).start())
+        each_sent(start_reduce, v)
+
+    combine(VIEWS - 1)
     for v in range(VIEWS):
         total = own[me, v]
         for d in range(1, n):
-            reduce_copy(d, v).wait_recv()
+            if d in (1, n - 1):
+                end = 0 if d == 1 else n - 1
+
+                @pl.when(me != end)
+                def _():
+                    reduce_copy(d, v).wait_recv()
+
+                @pl.when(me == end)
+                def _():
+                    parts_in[d, v] = jnp.zeros_like(parts_in[d, v])
+            else:
+                reduce_copy(d, v).wait_recv()
             total = total + parts_in[d, v].astype(F32)
         halo_s[2, v] = total.T.astype(BF16)
         exchange_start(halo_s.at[2, v], halo_s.at[2, v], halo_s, s_send, s_recv, v)
@@ -262,9 +318,13 @@
         across_copy(d, half).wait_send()
         forward_copy(d, core, 0, half).wait_send()
         forward_copy(d, core, 1, 1 - half).wait_send()
-        for v in range(VIEWS):
-            gather_copy(d, v, me).wait_send()
-            reduce_copy(d, v).wait_send()
+    for v in range(VIEWS):
+        each_sent(lambda d, v: gather_copy(d, v, me).wait_send(), v)
+        each_sent(lambda d, v: reduce_copy(d, v).wait_send(), v)
+        pl.when(me == 1)(lambda: relay_copy(v, 0, n - 1).wait_send())
+        pl.when(me == n - 2)(lambda: relay_copy(v, n - 1, 0).wait_send())
+        pl.when(me == 0)(lambda: extra_copy(v, n - 1, 1).wait_send())
+        pl.when(me == n - 1)(lambda: extra_copy(v, 0, n - 2).wait_send())
 
 
 def middle(volume, column_map, depth_map, measured, row_weight, band_start, band_len):
@@ -298,10 +358,12 @@
             pltpu.VMEM((n, *block), BF16),
             pltpu.VMEM((n, *block), F32),
             pltpu.VMEM((3, *block), BF16),
+            pltpu.VMEM(block, BF16),
             dma((slices // CHUNK,)), dma((views,)), dma((5,)),
             dma((n,)), dma((n,)), dma((n,)), dma((n,)), dma((2, n)), dma((2, n)),
             dma((2, views)), dma((2, views)), dma((views, n)), dma((views, n)),
             dma((views, n)), dma((views, n)), dma((2, views)), dma((2, views)),
+            dma((views,)), dma((views,)), dma((views,)),
         ],
         compiler_params=pltpu.CompilerParams(
             collective_id=0, has_side_effects=True, vmem_limit_bytes=GRANT

time: 33.4 us -> 36.6 us (1.096)
  Pallas kernels: 33.3 us -> 36.4 us
    pallas_call x1, Pallas kernels: 28.7 us -> 31.9 us  [middle(): pl.pallas_call(functools.partial(middle_kernel, n, groups), out_shape=jax...]
where the time goes in v4:
time: 36.6 us; the launch traced here: 36.5 us
  Pallas kernels  36.4 us (99%)
    pallas_call x1, Pallas kernels, middle(): pl.pallas_call(functools.partial(middle_kernel, n, groups), out_shape=jax...  31.9 us
    pallas_call x1, Pallas kernels, back(): pl.pallas_call(back_kernel, out_shape=jax.ShapeDtypeStruct(volume.shape,...  4.55 us

profile of v4, /device:TPU:1, one launch (start us, length us, event | category | flops | bytes accessed | tf_op | source)
XLA Modules:
  0.0 36.5 jit_solution(15618012749184578600)
XLA Ops:
  0.0 31.9 %project_and_spread.1.spread_in = bf16[3,2,128,128]{3,2,1,0:T(8,128)(2,1)} custom-call(s32[2,16]{1,0:T(2,128)} %starts.3, s32[2,16]{1,0:T(2,128)} %lens.3, f32[16,128,512]{2,1,0:T(8,128)} %volume.3, bf16[2,512,384]{2,1,0:T(8,128)(2,1)} %depth_in.1, bf16[2,128,2048]{2,1,0:T(8,128)(2,1)} %colmap.1, f32[1024,128]{1,0:T(8,128)} %bitcast.2, f32[1024,128]{1,0:T(8,128)} %bitcast.3), custom_call_target="tpu_custom_call" | custom-call | tf_op jit(solution)/shard_map/project_and_spread/pallas_call | solution.py:338
  31.9 4.6 %backproject.1 = f32[16,128,512]{2,1,0:T(8,128)} custom-call(s32[2,16]{1,0:T(2,128)} %starts.3, s32[2,16]{1,0:T(2,128)} %lens.3, bf16[3,2,128,128]{3,2,1,0:T(8,128)(2,1)} %project_and_spread.1.spread_in, bf16[2,512,384]{2,1,0:T(8,128)(2,1)} %depth_in.1, f32[16,128,512]{2,1,0:T(8,128)} %volume.3, bf16[16,128,512]{2,1,0:T(8,128)(2,1)} %col_weight.1), custom_call_target="tpu_custom_call" | custom-call | tf_op jit(solution)/shard_map/backproject/pallas_call | solution.py:452

commit v5 on v4

--- a/solution.py
+++ b/solution.py
@@ -20,9 +20,9 @@
     n, groups,
     starts, lens, volume, depth, colmap, measured, weight,
     out_ref,
-    start_ref, len_ref, vol, dcat, maps, meas, rw, meas_t, rw_t, acc, wt, halo, gathered, part, parts_in, own, halo_s, extra,
+    start_ref, len_ref, vol, dcat, maps, meas, rw, meas_t, rw_t, acc, wt, halo, gathered, part, parts_in, own, halo_s,
     vol_sem, dep_sem, loc_sem,
-    m_send, m_recv, x_send, x_recv, f_send, f_recv, h_send, h_recv, g_send, g_recv, r_send, r_recv, s_send, s_recv, relay_send, e_send, e_recv,
+    m_send, m_recv, x_send, x_recv, f_send, f_recv, h_send, h_recv, g_send, g_recv, r_send, r_recv, s_send, s_recv,
 ):
     g = lax.axis_index("gz")
     me = lax.axis_index("gx")
@@ -42,6 +42,19 @@
     def x_rows(who):
         return pl.ds(pl.multiple_of(who * BLK, BLK), BLK)
 
+    barrier = pltpu.get_barrier_semaphore()
+    for d in range(1, n):
+        pl.semaphore_signal(barrier, inc=1, device_id={"gx": lax.rem(me + d, n)}, device_id_type=MESH)
+
+    @pl.when(g > 0)
+    def _():
+        pl.semaphore_signal(barrier, inc=1, device_id={"gz": g - 1}, device_id_type=MESH)
+
+    @pl.when(g < groups - 1)
+    def _():
+        pl.semaphore_signal(barrier, inc=1, device_id={"gz": g + 1}, device_id_type=MESH)
+
+    pl.semaphore_signal(barrier, inc=1, device_id={"gz": across}, device_id_type=MESH)
     depth_copies = [
         pltpu.make_async_copy(depth.at[v], dcat.at[:, pl.ds(v * t_len, t_len)], dep_sem.at[v])
         for v in range(VIEWS)
@@ -70,19 +83,6 @@
     for copy in local_copies:
         copy.start()
 
-    barrier = pltpu.get_barrier_semaphore()
-    for d in range(1, n):
-        pl.semaphore_signal(barrier, inc=1, device_id={"gx": lax.rem(me + d, n)}, device_id_type=MESH)
-
-    @pl.when(g > 0)
-    def _():
-        pl.semaphore_signal(barrier, inc=1, device_id={"gz": g - 1}, device_id_type=MESH)
-
-    @pl.when(g < groups - 1)
-    def _():
-        pl.semaphore_signal(barrier, inc=1, device_id={"gz": g + 1}, device_id_type=MESH)
-
-    pl.semaphore_signal(barrier, inc=1, device_id={"gz": across}, device_id_type=MESH)
     below = jnp.where(g > 0, 1, 0)
     above = jnp.where(g < groups - 1, 1, 0)
     pl.semaphore_wait(barrier, n + below + above)
@@ -165,21 +165,9 @@
             device_id={"gx": lax.rem(me + d, n)}, device_id_type=MESH,
         )
 
-    def relay_copy(v, end, other):
-        return pltpu.make_async_remote_copy(
-            src_ref=gathered.at[other, v], dst_ref=gathered.at[other, v],
-            send_sem=relay_send.at[v], recv_sem=g_recv.at[v, (end - other) % n],
-            device_id={"gx": end}, device_id_type=MESH,
-        )
-
     def each_sent(do, v):
         for d in range(1, n):
-            if d == n - 1:
-                pl.when(me != 0)(functools.partial(do, d, v))
-            elif d == 1:
-                pl.when(me != n - 1)(functools.partial(do, d, v))
-            else:
-                do(d, v)
+            do(d, v)
 
     acc[...] = jnp.zeros_like(acc)
     for copy in depth_copies + band_copies:
@@ -215,11 +203,11 @@
         gathered[me, v] = (window + halo[0, v].astype(F32) + halo[1, v].astype(F32)).astype(BF16)
         each_sent(lambda d, v: gather_copy(d, v, me).start(), v)
 
-    send_window(0)
     for d in range(1, n):
         map_copy(d).wait_recv()
         across_copy(d, half).start()
         forward_copy(d, core, 0, half).start()
+    send_window(0)
     send_window(1)
     for copy in local_copies:
         copy.wait()
@@ -238,45 +226,13 @@
             device_id={"gx": peer}, device_id_type=MESH,
         )
 
-    def extra_copy(v, target, neighbour):
-        return pltpu.make_async_remote_copy(
-            src_ref=part.at[target, v], dst_ref=extra.at[v],
-            send_sem=e_send.at[v], recv_sem=e_recv.at[v],
-            device_id={"gx": neighbour}, device_id_type=MESH,
-        )
-
-    def start_reduce(d, v):
-        if d == n - 2 and d == 2:
-            pl.when(jnp.logical_and(me != 1, me != n - 2))(lambda: reduce_copy(d, v).start())
-        elif d == n - 2:
-            pl.when(me != 1)(lambda: reduce_copy(d, v).start())
-        elif d == 2:
-            pl.when(me != n - 2)(lambda: reduce_copy(d, v).start())
-        else:
-            reduce_copy(d, v).start()
-
-    def combine(v):
-        for device, target, d in ((1, n - 1, n - 2), (n - 2, 0, 2)):
-            @pl.when(me == device)
-            def _():
-                extra_copy(v, target, 0).wait_recv()
-                part[target, v] = (own[target, v] + extra[v].astype(F32)).astype(BF16)
-                reduce_copy(d, v).start()
-
-    for v in range(VIEWS):
-        first = sorted({2, n - 2})
-        for d in first + [d for d in range(1, n) if d not in first]:
+    for v in range(VIEWS):
+        for d in range(1, n):
             gather_copy(d, v, lax.rem(me - d + n, n)).wait_recv()
-            if d == 2:
-                pl.when(me == 1)(lambda: relay_copy(v, 0, n - 1).start())
-            if d == n - 2:
-                pl.when(me == n - 2)(lambda: relay_copy(v, n - 1, 0).start())
         if v == 0:
             for d in range(1, n):
                 forward_copy(d, 1 - core, 0, half).wait_recv()
                 forward_copy(d, 1 - core, 1, 1 - half).wait_recv()
-        else:
-            combine(v - 1)
         window = jnp.concatenate([gathered[j, v] for j in range(n)], axis=1)
         projection = jnp.dot(window, maps[v], preferred_element_type=F32)
         residual = (rw_t[v] * (meas_t[v] - projection)).astype(BF16)
@@ -284,26 +240,12 @@
         for j in range(n):
             own[j, v] = spread[:, j * BLK:(j + 1) * BLK]
             part[j, v] = spread[:, j * BLK:(j + 1) * BLK].astype(BF16)
-        pl.when(me == 0)(lambda: extra_copy(v, n - 1, 1).start())
-        pl.when(me == n - 1)(lambda: extra_copy(v, 0, n - 2).start())
-        each_sent(start_reduce, v)
-
-    combine(VIEWS - 1)
+        each_sent(lambda d, v: reduce_copy(d, v).start(), v)
+
     for v in range(VIEWS):
         total = own[me, v]
         for d in range(1, n):
-            if d in (1, n - 1):
-                end = 0 if d == 1 else n - 1
-
-                @pl.when(me != end)
-                def _():
-                    reduce_copy(d, v).wait_recv()
-
-                @pl.when(me == end)
-                def _():
-                    parts_in[d, v] = jnp.zeros_like(parts_in[d, v])
-            else:
-                reduce_copy(d, v).wait_recv()
+            reduce_copy(d, v).wait_recv()
             total = total + parts_in[d, v].astype(F32)
         halo_s[2, v] = total.T.astype(BF16)
         exchange_start(halo_s.at[2, v], halo_s.at[2, v], halo_s, s_send, s_recv, v)
@@ -321,10 +263,6 @@
     for v in range(VIEWS):
         each_sent(lambda d, v: gather_copy(d, v, me).wait_send(), v)
         each_sent(lambda d, v: reduce_copy(d, v).wait_send(), v)
-        pl.when(me == 1)(lambda: relay_copy(v, 0, n - 1).wait_send())
-        pl.when(me == n - 2)(lambda: relay_copy(v, n - 1, 0).wait_send())
-        pl.when(me == 0)(lambda: extra_copy(v, n - 1, 1).wait_send())
-        pl.when(me == n - 1)(lambda: extra_copy(v, 0, n - 2).wait_send())
 
 
 def middle(volume, column_map, depth_map, measured, row_weight, band_start, band_len):
@@ -358,12 +296,10 @@
             pltpu.VMEM((n, *block), BF16),
             pltpu.VMEM((n, *block), F32),
             pltpu.VMEM((3, *block), BF16),
-            pltpu.VMEM(block, BF16),
             dma((slices // CHUNK,)), dma((views,)), dma((5,)),
             dma((n,)), dma((n,)), dma((n,)), dma((n,)), dma((2, n)), dma((2, n)),
             dma((2, views)), dma((2, views)), dma((views, n)), dma((views, n)),
             dma((views, n)), dma((views, n)), dma((2, views)), dma((2, views)),
-            dma((views,)), dma((views,)), dma((views,)),
         ],
         compiler_params=pltpu.CompilerParams(
             collective_id=0, has_side_effects=True, vmem_limit_bytes=GRANT

time: 36.6 us -> 33.1 us (0.904)
  Pallas kernels: 36.4 us -> 33 us
    pallas_call x1, Pallas kernels: 31.9 us -> 28.4 us  [middle(): pl.pallas_call(functools.partial(middle_kernel, n, groups), out_shape=jax...]
where the time goes in v5:
time: 33.1 us; the launch traced here: 33 us
  Pallas kernels  33 us (100%)
    pallas_call x1, Pallas kernels, middle(): pl.pallas_call(functools.partial(middle_kernel, n, groups), out_shape=jax...  28.4 us
    pallas_call x1, Pallas kernels, back(): pl.pallas_call(back_kernel, out_shape=jax.ShapeDtypeStruct(volume.shape,...  4.56 us

profile of v5, /device:TPU:1, one launch (start us, length us, event | category | flops | bytes accessed | tf_op | source)
XLA Modules:
  0.0 33.0 jit_solution(10848439496264862954)
XLA Ops:
  0.0 28.4 %project_and_spread.1.spread_in = bf16[3,2,128,128]{3,2,1,0:T(8,128)(2,1)} custom-call(s32[2,16]{1,0:T(2,128)} %starts.3, s32[2,16]{1,0:T(2,128)} %lens.3, f32[16,128,512]{2,1,0:T(8,128)} %volume.3, bf16[2,512,384]{2,1,0:T(8,128)(2,1)} %depth_in.1, bf16[2,128,2048]{2,1,0:T(8,128)(2,1)} %colmap.1, f32[1024,128]{1,0:T(8,128)} %bitcast.2, f32[1024,128]{1,0:T(8,128)} %bitcast.3), custom_call_target="tpu_custom_call" | custom-call | tf_op jit(solution)/shard_map/project_and_spread/pallas_call | solution.py:276
  28.4 4.6 %backproject.1 = f32[16,128,512]{2,1,0:T(8,128)} custom-call(s32[2,16]{1,0:T(2,128)} %starts.3, s32[2,16]{1,0:T(2,128)} %lens.3, bf16[3,2,128,128]{3,2,1,0:T(8,128)(2,1)} %project_and_spread.1.spread_in, bf16[2,512,384]{2,1,0:T(8,128)(2,1)} %depth_in.1, f32[16,128,512]{2,1,0:T(8,128)} %volume.3, bf16[16,128,512]{2,1,0:T(8,128)(2,1)} %col_weight.1), custom_call_target="tpu_custom_call" | custom-call | tf_op jit(solution)/shard_map/backproject/pallas_call | solution.py:388
